TPU v7x, 256 devices: a whole 4x4x8 slice. The times are simulated.
256 devices in a mesh: panel: 2 (over core), rad: 4 (over z_lo), hor: 32 (over y, x, z_hi).
Axes of the slice: x: 4, y: 4, z: 8 (z_hi: 2, z_lo: 4; z = z_hi * 4 + z_lo), core: 2. Of those that a mesh axis runs over, the one named last changes fastest.
Arguments:
- final_cotangent: float32 [2, 8, 4, 256, 2304], P('panel', None, 'rad', 'hor'), may hold values from -6 to 6
- diffusivity: float32 [2, 4, 256, 2304], P('panel', 'rad', 'hor'), may hold values from 0.3 to 1.5
- theta_velocity: float32 [2, 4, 256, 2304], P('panel', 'rad', 'hor'), may hold values from -2.5 to 2.5
- phi_velocity: float32 [2, 4, 256, 2304], P('panel', 'rad', 'hor'), may hold values from -2.5 to 2.5
- radial_stencil: float32 [3, 8, 4], replicated, may hold values from -1 to 1
- field_coupling: float32 [4, 8, 8], replicated, may hold values from -2.5 to 2.5
- slot_targets: int32 [2, 32, 896], P('panel', 'hor'), may hold values from 0 to 5119, as said below
- slot_donors: int32 [2, 32, 896], P('panel', 'hor'), may hold values from 0 to 18431, as said below
- slot_weights: float32 [2, 32, 896], P('panel', 'hor'), may hold values from 0.1 to 0.4
- slot_counts: int32 [2, 32], P('panel', 'hor'), may hold values from 576 to 832, as said below
Outputs:
- initial_adjoint: float32 [2, 8, 4, 256, 2304], P('panel', None, 'rad', 'hor')
Inputs may be any that keep to these rules, and one draw needn't show every extreme that they name: `slot_targets`: each cell of the first and last rows of a panel is the target of four slots, all in the list of the donor tile s whose index times 2304 / 32 is at most its column and whose next index times 2304 / 32 is above it; each cell of the first and last columns is the target of four slots in the list of one donor tile, and 8 consecutive donor tiles, starting at a tile drawn for each panel, hold these, each for 32 rows in order; live slots come first, the four slots of a cell side by side. `slot_donors`: the four donors of a cell are the corners of a two by two block of cells of one donor tile; for the first cell of every list this block is the tile's last two rows and last two columns. `slot_counts`: A donor tile's list holds 576 live slots, plus 32 * 8 if it is one of the 8 tiles that hold the first and last columns' cells.
All inputs are finite; a program needn't handle non-finite values.
Results may differ from a plain program's by a relative error of at most 0.00005.
Values sent between devices are 32-bit elements; how exact they have to be, the bound alone decides.
A program may use at most 128 MiB of HBM per device.

v0:
```python
import jax
import jax.numpy as jnp
from jax import lax
from jax.sharding import PartitionSpec as P

STEP_SIZE = 0.2


def extended(x, sides, width):
    edges = {}
    for axis, dim in sides:
        peers, length = (lax.axis_size(axis), x.shape[dim])
        up = [(i, (i + 1) % peers) for i in range(peers - 1)]
        last = lax.slice_in_dim(x, length - width, length, axis=dim)
        initial = lax.slice_in_dim(x, 0, width, axis=dim)
        edges[dim] = (
            lax.ppermute(last, axis, up),
            lax.ppermute(initial, axis, [(b, a) for a, b in up]),
        )
    done = []
    for _, dim in sides:
        low, high = edges[dim]
        around = [(width, width) if d in done else (0, 0) for d in range(x.ndim)]
        x = jnp.concatenate([jnp.pad(low, around), x, jnp.pad(high, around)], axis=dim)
        done.append(dim)
    return x


def rows_for(lines, peers):
    spare = -lines.shape[0] % peers
    if not spare:
        return lines
    return jnp.concatenate([lines, jnp.zeros((spare, *lines.shape[1:]), lines.dtype)])


def copy_for_each(x, axis):
    copies = jnp.broadcast_to(x, (lax.axis_size(axis), *x.shape))
    return lax.all_to_all(copies, axis, split_axis=0, concat_axis=0, tiled=True)


def laid_out(parts, dim):
    parts = jnp.moveaxis(parts, 0, dim)
    lengths = parts.shape
    return parts.reshape(*lengths[:dim], lengths[dim] * lengths[dim + 1], *lengths[dim + 2 :])


def gather_directly(x, axis, dim):
    parts = copy_for_each(x, axis)
    return laid_out(parts, dim)


def cut_along(x, dim, peers):
    before, after = (x.shape[:dim], x.shape[dim + 1 :])
    return jnp.moveaxis(x.reshape(*before, peers, -1, *after), dim, 0)


def summed_on_arrival(x, axis, dim):
    parts = cut_along(x, dim, lax.axis_size(axis))
    arrived = lax.all_to_all(parts, axis, split_axis=0, concat_axis=0, tiled=True)
    return arrived.sum(axis=0)


def sum_by_parts(x, axes):
    padded = rows_for(x, lax.axis_size(axes))
    whole = gather_directly(summed_on_arrival(padded, axes, 0), axes, 0)
    return lax.slice_in_dim(whole, 0, len(x)).reshape(x.shape)


def in_one(arrays, axis):
    vector, at, gathered = (jnp.concatenate([a.reshape(-1) for a in arrays]), 0, [])
    subtotal = sum_by_parts(vector, axis)
    for a in arrays:
        gathered.append(subtotal[at : at + a.size].reshape(a.shape))
        at += a.size
    return tuple(gathered)


def partner(x, axis, bit):
    return lax.ppermute(x, axis, [(i, i ^ 1 << bit) for i in range(lax.axis_size(axis))])


def body(
    final_cotangent,
    diffusivity,
    theta_velocity,
    phi_velocity,
    radial_stencil,
    field_coupling,
    slot_targets,
    slot_donors,
    slot_weights,
    slot_counts,
):
    fields, levels, rows, columns = final_cotangent.shape[1:]
    stacked = fields * levels
    cells = rows * columns
    tiles = lax.axis_size("hor")
    total_rows = rows * tiles
    tile_index = lax.axis_index("hor")
    level_start = lax.axis_index("rad") * levels
    diffuse = diffusivity[0]
    theta_flow = theta_velocity[0]
    phi_flow = phi_velocity[0]
    coef_north = diffuse + theta_flow
    coef_south = diffuse - theta_flow
    coef_east = diffuse + phi_flow
    coef_west = diffuse - phi_flow
    center = 4.0 * diffuse
    padded_stencil = jnp.pad(radial_stencil, ((0, 0), (0, 0), (1, 1)))
    diag_here = lax.dynamic_slice_in_dim(padded_stencil[0], level_start + 1, levels, 1)[
        :, :, None, None
    ]
    upper_below = lax.dynamic_slice_in_dim(padded_stencil[1], level_start, levels, 1)[
        :, :, None, None
    ]
    lower_above = lax.dynamic_slice_in_dim(padded_stencil[2], level_start + 2, levels, 1)[
        :, :, None, None
    ]
    coupling_here = lax.dynamic_slice_in_dim(field_coupling, level_start, levels, 0)
    row_global = tile_index * rows + jnp.arange(rows, dtype=jnp.int32)[:, None]
    col_ids = jnp.arange(columns, dtype=jnp.int32)[None, :]
    border = (
        (row_global == 0)
        | (row_global == total_rows - 1)
        | (col_ids == 0)
        | (col_ids == columns - 1)
    )
    target_index = slot_targets[0, 0]
    donor_index = slot_donors[0, 0]
    weights = slot_weights[0, 0]
    count = slot_counts[0, 0]
    slot_ids = jnp.arange(target_index.shape[0], dtype=jnp.int32)
    live_weights = jnp.where(slot_ids < count, weights, jnp.float32(0.0))

    def transpose_operator(cotangent):
        padded = extended(cotangent, (("rad", 1), ("hor", 2)), 1)
        level_mid = padded[:, 1:-1]
        row_below = level_mid[:, :, :-2]
        row_above = level_mid[:, :, 2:]
        col_before = jnp.pad(cotangent, ((0, 0), (0, 0), (0, 0), (1, 0)))[..., :-1]
        col_after = jnp.pad(cotangent, ((0, 0), (0, 0), (0, 0), (0, 1)))[..., 1:]
        horizontal = (
            coef_south * row_below
            + coef_north * row_above
            + coef_west * col_before
            + coef_east * col_after
            - center * cotangent
        )
        radial = (
            diag_here * cotangent
            + upper_below * padded[:, :-2, 1:-1]
            + lower_above * padded[:, 2:, 1:-1]
        )
        coupled = jnp.einsum(
            "rfe,frij->erij", coupling_here, cotangent, precision=lax.Precision.HIGHEST
        )
        return horizontal + radial + coupled

    def border_table(cotangent):
        block = cotangent.reshape(stacked, rows, columns)
        sides = jnp.stack([block[:, :, 0], block[:, :, columns - 1]], axis=1)
        first_row = jnp.where(tile_index == 0, block[:, 0, :], jnp.float32(0.0))
        last_row = jnp.where(tile_index == tiles - 1, block[:, rows - 1, :], jnp.float32(0.0))
        edges = jnp.stack([first_row, last_row], axis=1)
        placed = lax.dynamic_update_slice(
            jnp.zeros((stacked, 2, total_rows), jnp.float32),
            sides,
            (jnp.int32(0), jnp.int32(0), tile_index * rows),
        )
        edges, sides = in_one((edges, placed), "hor")
        edges, sides = partner((edges, sides), "panel", 0)
        return jnp.concatenate(
            [edges.reshape(stacked, 2 * columns), sides.reshape(stacked, 2 * total_rows)], axis=1
        )

    def transpose_overset(cotangent):
        kept = jnp.where(border, jnp.float32(0.0), cotangent).reshape(stacked, cells)
        table = border_table(cotangent)
        values = jnp.take(table, target_index, axis=1) * live_weights[None]
        return kept.at[:, donor_index].add(values).reshape(cotangent.shape)

    cotangent = final_cotangent[0]
    after_full = transpose_overset(cotangent)
    pulled = STEP_SIZE * transpose_operator(after_full)
    after_half = transpose_overset(pulled)
    result = after_full + after_half + 0.5 * STEP_SIZE * transpose_operator(after_half)
    return result[None]


def solution(mesh):
    return jax.shard_map(
        body,
        mesh=mesh,
        in_specs=(
            P("panel", None, "rad", "hor", None),
            P("panel", "rad", "hor", None),
            P("panel", "rad", "hor", None),
            P("panel", "rad", "hor", None),
            P(),
            P(),
            P("panel", "hor", None),
            P("panel", "hor", None),
            P("panel", "hor", None),
            P("panel", "hor"),
        ),
        out_specs=P("panel", None, "rad", "hor", None),
        check_vma=False,
    )
```

profile of v0, /device:TPU:32, one launch (start us, length us, event | category | flops | bytes accessed | tf_op | source)
XLA Modules:
  0.0 234.8 jit_solution(15183477471996289330)
XLA Ops:
  0.0 1.3 copy.223
  2.9 14.1 %all-to-all-start = ((f32[32,1,1280]{2,1,0:T(1,128)}), f32[32,1,1280]{2,1,0:T(1,128)S(1)}, u32[]{:S(2)}, u32[]{:S(2)}) async-start(f32[32,1,1280]{2,1,0:T(1,128)} %bitcast.5), calls=%async_computation | async-start | bytes 327680 | tf_op jit(solution)/shard_map/all_to_all | solution.py:59
  17.0 6.1 %copy.144 = f32[1,8,1,8,2304]{1,4,3,2,0:T(8,128)} copy(f32[1,8,1,8,2304]{4,3,2,1,0:T(8,128)} %param.12) | data formatting | bytes 1179648 | tf_op args[0]
  24.1 11.7 %bitcast_select_fusion = f32[8,18432]{0,1:T(8,128)} fusion(f32[1,8,1,8,2304]{1,4,3,2,0:T(8,128)} %copy.144, pred[18432]{0:T(1024)(128)(4,1)S(1)} %or.41), kind=kLoop, calls=%fused_computation.4 | loop fusion | flops 147456 | bytes 1198080 | tf_op jit(solution)/shard_map/jit(_where)/select_n | solution.py:177
  36.6 0.8 broadcast_in_dim.65
  37.4 12.2 %all-to-all-start.1 = ((f32[32,1,1280]{2,1,0:T(1,128)}), f32[32,1,1280]{2,1,0:T(1,128)S(1)}, u32[]{:S(2)}, u32[]{:S(2)}) async-start(f32[32,1,1280]{2,1,0:T(1,128)} %broadcast_in_dim.65), calls=%async_computation.1 | async-start | bytes 327680 | tf_op jit(solution)/shard_map/all_to_all | solution.py:38
  49.6 12.8 %all-to-all-done.1 = f32[32,1,1280]{2,1,0:T(1,128)S(1)} async-done(((f32[32,1,1280]{2,1,0:T(1,128)}), f32[32,1,1280]{2,1,0:T(1,128)S(1)}, u32[]{:S(2)}, u32[]{:S(2)}) %all-to-all-start.1) | async-done | bytes 163872 | tf_op jit(solution)/shard_map/all_to_all | solution.py:38
  63.7 0.8 collective-permute-done.1
  65.3 17.0 %scatter_custom_fusion = f32[8,18432]{0,1:T(8,128)} fusion(f32[8,18432]{0,1:T(8,128)} %bitcast_select_fusion, s32[896]{0:T(1024)S(1)} %fusion.49, f32[]{:T(128)} %constant.16.clone.2, f32[896]{0:T(1024)S(1)} %fusion.46, pred[896]{0:T(1024)(128)(4,1)S(1)} %compare_and_fusion, f32[8,5120]{0,1:T(8,128)S(1)} %copy.151, s32[1024]{0:T(1024)S(1)} %pad_clamp_fusion), kind=kCustom, calls=%fused_computation.57 | custom fusion | flops 21504 | bytes 3220992 | tf_op jit(solution)/shard_map/scatter-add | solution.py:180
  82.3 5.5 %copy.172 = f32[8,1,8,2304]{3,0,2,1:T(8,128)S(1)} copy(f32[8,1,8,2304]{0,3,2,1:T(8,128)} %bitcast.97) | data formatting | bytes 1179648 | tf_op jit(solution)/shard_map/reshape | solution.py:180
  87.9 2.9 %collective-permute-start.4 = (f32[8,1,8,2304]{3,0,2,1:T(8,128)S(1)}, f32[8,1,8,2304]{3,0,2,1:T(8,128)S(1)}, u32[]{:S(2)}, u32[]{:S(2)}) collective-permute-start(f32[8,1,8,2304]{3,0,2,1:T(8,128)S(1)} %copy.172), channel_id=1, source_target_pairs={{32,0},{64,32},{96,64},{33,1},{65,33},{97,65},{34,2},{66,34},{98,6... | collective-permute-start | bytes 1769480 | tf_op jit(solution)/shard_map/ppermute | solution.py:18
  90.8 2.9 %collective-permute-start.3 = (f32[8,1,8,2304]{3,0,2,1:T(8,128)S(1)}, f32[8,1,8,2304]{3,0,2,1:T(8,128)S(1)}, u32[]{:S(2)}, u32[]{:S(2)}) collective-permute-start(f32[8,1,8,2304]{3,0,2,1:T(8,128)S(1)} %copy.172), channel_id=1, source_target_pairs={{0,32},{32,64},{64,96},{1,33},{33,65},{65,97},{2,34},{34,66},{66,9... | collective-permute-start | bytes 1769480 | tf_op jit(solution)/shard_map/ppermute | solution.py:17
  93.7 2.6 %collective-permute-start.2 = (f32[8,1,1,2304]{3,0,2,1:T(8,128)S(1)}, f32[8,1,1,2304]{3,0,2,1:T(8,128)S(1)}, u32[]{:S(2)}, u32[]{:S(2)}) collective-permute-start(f32[8,1,1,2304]{3,0,2,1:T(8,128)S(1)} %get-tuple-element.12), channel_id=1, source_target_pairs={{0,1},{1,2},{2,3},{3,4},{4,5},{5,6},{6,7},{7,8},{8,9},{9,10},{10,1... | collective-permute-start | bytes 221192 | tf_op jit(solution)/shard_map/ppermute | solution.py:17
  96.3 1.5 collective-permute-start.5
  97.8 7.8 %collective-permute-done.2 = f32[8,1,1,2304]{3,0,2,1:T(8,128)S(1)} collective-permute-done((f32[8,1,1,2304]{3,0,2,1:T(8,128)S(1)}, f32[8,1,1,2304]{3,0,2,1:T(8,128)S(1)}, u32[]{:S(2)}, u32[]{:S(2)}) %collective-permute-start.2) | collective-permute-done | bytes 73760 | tf_op jit(solution)/shard_map/ppermute | solution.py:17
  105.6 5.7 %collective-permute-done.5 = f32[8,1,1,2304]{3,0,2,1:T(8,128)S(1)} collective-permute-done((f32[8,1,1,2304]{3,0,2,1:T(8,128)S(1)}, f32[8,1,1,2304]{3,0,2,1:T(8,128)S(1)}, u32[]{:S(2)}, u32[]{:S(2)}) %collective-permute-start.5) | collective-permute-done | bytes 73760 | tf_op jit(solution)/shard_map/ppermute | solution.py:18
  111.3 10.8 %broadcast_select_fusion = (f32[8,1,8,2304]{3,0,2,1:T(8,128)S(1)}, f32[8,1,8,2304]{3,0,2,1:T(8,128)S(1)}) fusion(pred[8,2304]{1,0:T(8,128)(4,1)S(1)} %or_or_fusion, f32[8,8,2304]{0,2,1:T(8,128)} %bitcast.98, f32[4,8,8]{2,1,0:T(8,128)S(1)} %copy-done, s32[]{:T(128)S(6)} %select_n.89, f32[8,1,8,2304]{3,0,2,1:T(8,128)S(1)} %collective-permute-done.4, ...), kind=kOutput, calls=%fused_computation.62 | convolution fusion | flops 18579456 | bytes 4079108 | tf_op jit(solution)/shard_map/rfe,frij->erij/dot_general | solution.py:154
  123.1 23.7 %all_to_all.31 = f32[32,1,1280]{2,1,0:T(1,128)S(1)} all-to-all(f32[32,1,1280]{2,1,0:T(1,128)S(1)} %bitcast.108), channel_id=1, replica_groups=mesh['panel'=2,'rad'=4,'hor'=32] {'hor'}, dimensions={0} | all-to-all | bytes 327680 | tf_op jit(solution)/shard_map/all_to_all | solution.py:59
  147.0 16.3 %all_to_all.30 = f32[32,1,1280]{2,1,0:T(1,128)S(1)} all-to-all(f32[32,1,1280]{2,1,0:T(1,128)S(1)} %broadcast_in_dim.69), channel_id=1, replica_groups=mesh['panel'=2,'rad'=4,'hor'=32] {'hor'}, dimensions={0} | all-to-all | bytes 327680 | tf_op jit(solution)/shard_map/all_to_all | solution.py:38
  164.0 0.8 collective-permute-start.7
  164.8 5.0 %copy.170 = f32[8,18432]{0,1:T(8,128)} copy(f32[8,18432]{1,0:T(8,128)S(1)} %bitcast.101) | data formatting | bytes 1179648 | tf_op jit(solution)/shard_map/reshape | solution.py:177
  170.6 1.6 copy.169
  172.2 17.0 %scatter_custom_fusion.1 = f32[8,18432]{0,1:T(8,128)} fusion(f32[8,18432]{0,1:T(8,128)} %copy.170, s32[896]{0:T(1024)S(1)} %fusion.49, f32[]{:T(128)} %constant.16.clone.2, f32[896]{0:T(1024)S(1)} %fusion.46, pred[896]{0:T(1024)(128)(4,1)S(1)} %compare_and_fusion, f32[8,5120]{0,1:T(8,128)S(1)} %copy.169, s32[1024]{0:T(1024)S(1)} %pad_clamp_fusion), kind=kCustom, calls=%fused_computation.54 | custom fusion | flops 21504 | bytes 3220992 | tf_op jit(solution)/shard_map/scatter-add | solution.py:180
  189.3 5.5 %copy.173 = f32[8,1,8,2304]{3,0,2,1:T(8,128)S(1)} copy(f32[8,1,8,2304]{0,3,2,1:T(8,128)} %bitcast.99) | data formatting | bytes 1179648 | tf_op jit(solution)/shard_map/reshape | solution.py:180
  194.8 5.4 %collective-permute-start.9 = (f32[8,1,8,2304]{3,0,2,1:T(8,128)S(1)}, f32[8,1,8,2304]{3,0,2,1:T(8,128)S(1)}, u32[]{:S(2)}, u32[]{:S(2)}) collective-permute-start(f32[8,1,8,2304]{3,0,2,1:T(8,128)S(1)} %copy.173), channel_id=1, source_target_pairs={{0,32},{32,64},{64,96},{1,33},{33,65},{65,97},{2,34},{34,66},{66,9... | collective-permute-start | bytes 1769480 | tf_op jit(solution)/shard_map/ppermute | solution.py:17
  200.2 1.9 collective-permute-start.10
  202.2 3.1 %collective-permute-start.8 = (f32[8,1,1,2304]{3,0,2,1:T(8,128)S(1)}, f32[8,1,1,2304]{3,0,2,1:T(8,128)S(1)}, u32[]{:S(2)}, u32[]{:S(2)}) collective-permute-start(f32[8,1,1,2304]{3,0,2,1:T(8,128)S(1)} %get-tuple-element.6), channel_id=1, source_target_pairs={{0,1},{1,2},{2,3},{3,4},{4,5},{5,6},{6,7},{7,8},{8,9},{9,10},{10,1... | collective-permute-start | bytes 221192 | tf_op jit(solution)/shard_map/ppermute | solution.py:17
  205.3 1.3 collective-permute-start.11
  206.6 10.6 %collective-permute-done.8 = f32[8,1,1,2304]{3,0,2,1:T(8,128)S(1)} collective-permute-done((f32[8,1,1,2304]{3,0,2,1:T(8,128)S(1)}, f32[8,1,1,2304]{3,0,2,1:T(8,128)S(1)}, u32[]{:S(2)}, u32[]{:S(2)}) %collective-permute-start.8) | collective-permute-done | bytes 73760 | tf_op jit(solution)/shard_map/ppermute | solution.py:17
  217.2 5.6 %collective-permute-done.11 = f32[8,1,1,2304]{3,0,2,1:T(8,128)S(1)} collective-permute-done((f32[8,1,1,2304]{3,0,2,1:T(8,128)S(1)}, f32[8,1,1,2304]{3,0,2,1:T(8,128)S(1)}, u32[]{:S(2)}, u32[]{:S(2)}) %collective-permute-start.11) | collective-permute-done | bytes 73760 | tf_op jit(solution)/shard_map/ppermute | solution.py:18
  222.9 10.9 %fusion.16 = f32[1,8,1,8,2304]{4,1,3,2,0:T(8,128)S(1)} fusion(f32[8,1,8,2304]{3,0,2,1:T(8,128)S(1)} %copy.173, f32[8,1,1,2304]{3,0,2,1:T(8,128)S(1)} %collective-permute-done.11, f32[8,1,8,2304]{3,0,2,1:T(8,128)S(1)} %collective-permute-done.10, f32[8,1,8,2304]{3,0,2,1:T(8,128)S(1)} %collective-permute-done.9, ...), kind=kOutput, calls=%fused_computation.27 | convolution fusion | flops 18726912 | bytes 4060676 | tf_op jit(solution)/shard_map/rfe,frij->erij/dot_general | solution.py:154
  233.8 1.0 copy.185
  (94 shorter events, 7.1 us)
Async XLA Ops:
  0.0 111.3 %copy-start = (f32[4,8,8]{2,1,0:T(8,128)S(1)}, f32[4,8,8]{2,1,0:T(8,128)}, u32[]{:S(2)}) copy-start(f32[4,8,8]{2,1,0:T(8,128)} %param.17) | copy-start | bytes 3076
  0.0 23.8 %copy-start.7 = (s32[1,1,896]{2,1,0:T(1,128)S(1)}, s32[1,1,896]{2,1,0:T(1,128)}, u32[]{:S(2)}) copy-start(s32[1,1,896]{2,1,0:T(1,128)} %param.18) | copy-start | bytes 10756
  0.0 24.0 %copy-start.8 = (f32[1,1,896]{2,1,0:T(1,128)S(1)}, f32[1,1,896]{2,1,0:T(1,128)}, u32[]{:S(2)}) copy-start(f32[1,1,896]{2,1,0:T(1,128)} %param.20) | copy-start | bytes 10756
  2.9 33.6 %all-to-all-start = ((f32[32,1,1280]{2,1,0:T(1,128)}), f32[32,1,1280]{2,1,0:T(1,128)S(1)}, u32[]{:S(2)}, u32[]{:S(2)}) async-start(f32[32,1,1280]{2,1,0:T(1,128)} %bitcast.5), calls=%async_computation | async-start | bytes 327680 | tf_op jit(solution)/shard_map/all_to_all | solution.py:59
  24.1 11.8 %copy-start.3 = (f32[1,1,8,2304]{3,2,1,0:T(8,128)S(1)}, f32[1,1,8,2304]{3,2,1,0:T(8,128)}, u32[]{:S(2)}) copy-start(f32[1,1,8,2304]{3,2,1,0:T(8,128)} %param.13) | copy-start | bytes 221188
  24.1 11.7 %copy-start.4 = (f32[1,1,8,2304]{3,2,1,0:T(8,128)S(1)}, f32[1,1,8,2304]{3,2,1,0:T(8,128)}, u32[]{:S(2)}) copy-start(f32[1,1,8,2304]{3,2,1,0:T(8,128)} %param.14) | copy-start | bytes 221188
  24.1 11.7 %copy-start.5 = (f32[1,1,8,2304]{3,2,1,0:T(8,128)S(1)}, f32[1,1,8,2304]{3,2,1,0:T(8,128)}, u32[]{:S(2)}) copy-start(f32[1,1,8,2304]{3,2,1,0:T(8,128)} %param.15) | copy-start | bytes 221188
  24.1 12.4 %copy-start.9 = (s32[1,1,896]{2,1,0:T(1,128)S(1)}, s32[1,1,896]{2,1,0:T(1,128)}, u32[]{:S(2)}) copy-start(s32[1,1,896]{2,1,0:T(1,128)} %param.19) | copy-start | bytes 10756
  24.1 25.5 %copy-start.6 = (f32[3,8,4]{1,2,0:T(4,128)S(1)}, f32[3,8,4]{1,2,0:T(4,128)}, u32[]{:S(2)}) copy-start(f32[3,8,4]{1,2,0:T(4,128)} %param.16) | copy-start | bytes 1156
  37.4 25.0 %all-to-all-start.1 = ((f32[32,1,1280]{2,1,0:T(1,128)}), f32[32,1,1280]{2,1,0:T(1,128)S(1)}, u32[]{:S(2)}, u32[]{:S(2)}) async-start(f32[32,1,1280]{2,1,0:T(1,128)} %broadcast_in_dim.65), calls=%async_computation.1 | async-start | bytes 327680 | tf_op jit(solution)/shard_map/all_to_all | solution.py:38
  62.5 2.0 collective-permute-start
  63.1 1.4 collective-permute-start.1
  82.3 29.0 %copy-start.1 = (f32[8,2304]{1,0:T(8,128)S(1)}, f32[8,2304]{1,0:T(8,128)}, u32[]{:S(2)}) copy-start(f32[8,2304]{1,0:T(8,128)} %get-tuple-element.24) | copy-start | bytes 221188
  87.9 23.5 %collective-permute-start.4 = (f32[8,1,8,2304]{3,0,2,1:T(8,128)S(1)}, f32[8,1,8,2304]{3,0,2,1:T(8,128)S(1)}, u32[]{:S(2)}, u32[]{:S(2)}) collective-permute-start(f32[8,1,8,2304]{3,0,2,1:T(8,128)S(1)} %copy.172), channel_id=1, source_target_pairs={{32,0},{64,32},{96,64},{33,1},{65,33},{97,65},{34,2},{66,34},{98,6... | collective-permute-start | bytes 1769480 | tf_op jit(solution)/shard_map/ppermute | solution.py:18
  90.8 20.5 %collective-permute-start.3 = (f32[8,1,8,2304]{3,0,2,1:T(8,128)S(1)}, f32[8,1,8,2304]{3,0,2,1:T(8,128)S(1)}, u32[]{:S(2)}, u32[]{:S(2)}) collective-permute-start(f32[8,1,8,2304]{3,0,2,1:T(8,128)S(1)} %copy.172), channel_id=1, source_target_pairs={{0,32},{32,64},{64,96},{1,33},{33,65},{65,97},{2,34},{34,66},{66,9... | collective-permute-start | bytes 1769480 | tf_op jit(solution)/shard_map/ppermute | solution.py:17
  93.7 11.9 %collective-permute-start.2 = (f32[8,1,1,2304]{3,0,2,1:T(8,128)S(1)}, f32[8,1,1,2304]{3,0,2,1:T(8,128)S(1)}, u32[]{:S(2)}, u32[]{:S(2)}) collective-permute-start(f32[8,1,1,2304]{3,0,2,1:T(8,128)S(1)} %get-tuple-element.12), channel_id=1, source_target_pairs={{0,1},{1,2},{2,3},{3,4},{4,5},{5,6},{6,7},{7,8},{8,9},{9,10},{10,1... | collective-permute-start | bytes 221192 | tf_op jit(solution)/shard_map/ppermute | solution.py:17
  96.3 15.0 %collective-permute-start.5 = (f32[8,1,1,2304]{3,0,2,1:T(8,128)S(1)}, f32[8,1,1,2304]{3,0,2,1:T(8,128)S(1)}, u32[]{:S(2)}, u32[]{:S(2)}) collective-permute-start(f32[8,1,1,2304]{3,0,2,1:T(8,128)S(1)} %get-tuple-element.13), channel_id=1, source_target_pairs={{1,0},{2,1},{3,2},{4,3},{5,4},{6,5},{7,6},{8,7},{9,8},{10,9},{11,1... | collective-permute-start | bytes 221192 | tf_op jit(solution)/shard_map/ppermute | solution.py:18
  163.4 6.4 %collective-permute-start.6 = (f32[8,2,2304]{2,1,0:T(2,128)S(1)}, f32[8,2,2304]{2,1,0:T(2,128)S(1)}, u32[]{:S(2)}, u32[]{:S(2)}) collective-permute-start(f32[8,2,2304]{2,1,0:T(2,128)S(1)} %reshape.290), channel_id=1, source_target_pairs={{0,128},{128,0},{1,129},{129,1},{2,130},{130,2},{3,131},{131,3},{4... | collective-permute-start | bytes 442376 | tf_op jit(solution)/shard_map/ppermute | solution.py:79
  164.0 5.8 %collective-permute-start.7 = (f32[8,2,256]{2,1,0:T(2,128)S(1)}, f32[8,2,256]{2,1,0:T(2,128)S(1)}, u32[]{:S(2)}, u32[]{:S(2)}) collective-permute-start(f32[8,2,256]{2,1,0:T(2,128)S(1)} %slice.143), channel_id=1, source_target_pairs={{0,128},{128,0},{1,129},{129,1},{2,130},{130,2},{3,131},{131,3},{4... | collective-permute-start | bytes 49160 | tf_op jit(solution)/shard_map/ppermute | solution.py:79
  189.3 33.6 %copy-start.2 = (f32[8,2304]{1,0:T(8,128)S(1)}, f32[8,2304]{1,0:T(8,128)}, u32[]{:S(2)}) copy-start(f32[8,2304]{1,0:T(8,128)} %get-tuple-element.24) | copy-start | bytes 221188
  194.8 28.1 %collective-permute-start.9 = (f32[8,1,8,2304]{3,0,2,1:T(8,128)S(1)}, f32[8,1,8,2304]{3,0,2,1:T(8,128)S(1)}, u32[]{:S(2)}, u32[]{:S(2)}) collective-permute-start(f32[8,1,8,2304]{3,0,2,1:T(8,128)S(1)} %copy.173), channel_id=1, source_target_pairs={{0,32},{32,64},{64,96},{1,33},{33,65},{65,97},{2,34},{34,66},{66,9... | collective-permute-start | bytes 1769480 | tf_op jit(solution)/shard_map/ppermute | solution.py:17
  200.2 22.7 %collective-permute-start.10 = (f32[8,1,8,2304]{3,0,2,1:T(8,128)S(1)}, f32[8,1,8,2304]{3,0,2,1:T(8,128)S(1)}, u32[]{:S(2)}, u32[]{:S(2)}) collective-permute-start(f32[8,1,8,2304]{3,0,2,1:T(8,128)S(1)} %copy.173), channel_id=1, source_target_pairs={{32,0},{64,32},{96,64},{33,1},{65,33},{97,65},{34,2},{66,34},{98,6... | collective-permute-start | bytes 1769480 | tf_op jit(solution)/shard_map/ppermute | solution.py:18
  202.2 15.1 %collective-permute-start.8 = (f32[8,1,1,2304]{3,0,2,1:T(8,128)S(1)}, f32[8,1,1,2304]{3,0,2,1:T(8,128)S(1)}, u32[]{:S(2)}, u32[]{:S(2)}) collective-permute-start(f32[8,1,1,2304]{3,0,2,1:T(8,128)S(1)} %get-tuple-element.6), channel_id=1, source_target_pairs={{0,1},{1,2},{2,3},{3,4},{4,5},{5,6},{6,7},{7,8},{8,9},{9,10},{10,1... | collective-permute-start | bytes 221192 | tf_op jit(solution)/shard_map/ppermute | solution.py:17
  205.3 17.6 %collective-permute-start.11 = (f32[8,1,1,2304]{3,0,2,1:T(8,128)S(1)}, f32[8,1,1,2304]{3,0,2,1:T(8,128)S(1)}, u32[]{:S(2)}, u32[]{:S(2)}) collective-permute-start(f32[8,1,1,2304]{3,0,2,1:T(8,128)S(1)} %get-tuple-element.7), channel_id=1, source_target_pairs={{1,0},{2,1},{3,2},{4,3},{5,4},{6,5},{7,6},{8,7},{9,8},{10,9},{11,1... | collective-permute-start | bytes 221192 | tf_op jit(solution)/shard_map/ppermute | solution.py:18
where the time goes:
time: 236 us; the launch traced here: 235 us
  starting transfers between devices  49.5 us (21%)
  other arithmetic  49 us (21%)
  waiting for transfers between devices  43.4 us (18%)
  blocking collectives  40 us (17%)
  local copies, waits for them, and re-layouts  29.9 us (13%)
  matrix products  21.7 us (9%)
    scatter-add x2, other arithmetic, transpose_overset(): return kept.at[:, donor_index].add(values).reshape(cotangent.shape)  34 us
    all_to_all x1, blocking collectives, summed_on_arrival(): lax.all_to_all(parts, axis, split_axis=0, concat_axis=0, tiled=True)  23.7 us
    dot_general x2, matrix products, transpose_operator(): jnp.einsum('rfe,frij->erij', coupling_here, cotangent, precision=lax.Prec...  21.7 us
    ppermute x4, waiting for transfers between devices, extended(): lax.ppermute(last, axis, up)  18.4 us
    all_to_all x1, blocking collectives, copy_for_each(): return lax.all_to_all(copies, axis, split_axis=0, concat_axis=0, tiled=True)  16.3 us
    all_to_all x1, starting transfers between devices, summed_on_arrival(): lax.all_to_all(parts, axis, split_axis=0, concat_axis=0, tiled=True)  14.1 us
    ppermute x4, starting transfers between devices, extended(): lax.ppermute(last, axis, up)  14.1 us
    all_to_all x1, waiting for transfers between devices, copy_for_each(): return lax.all_to_all(copies, axis, split_axis=0, concat_axis=0, tiled=True)  12.8 us
  transfers between devices with their start and end apart: 14, of which 6 were waited for; matrix products, arithmetic and copies ran while one was open for 11% of the time, Pallas kernels for 0%

commit v1 on v0

v1 whole, which is shorter than its diff:
```python
import functools

import jax
import jax.numpy as jnp
from jax import lax
from jax.experimental import pallas as pl
from jax.experimental.pallas import tpu as pltpu
from jax.sharding import PartitionSpec as P

STEP_SIZE = 0.2
MESH = pl.DeviceIdType.MESH
F32 = jnp.float32
BF16 = jnp.bfloat16
BLK = 256


def split(x):
    hi = x.astype(BF16)
    lo = (x - hi.astype(F32)).astype(BF16)
    return hi, lo


def kernel(
    tiles,
    levels,
    c_ref,
    kap_ref,
    vt_ref,
    vp_ref,
    rs_ref,
    fc_ref,
    tgt_ref,
    don_ref,
    wt_ref,
    cnt_ref,
    out_ref,
    w_ref,
    v_ref,
    rad_buf,
    hal_send,
    hal_recv,
    side_msg,
    side_buf,
    row_line,
    pieces,
    row_buf,
    val_send,
    val_recv,
    gather_rows,
    gather_sides,
    side_group,
    key_ref,
    live_ref,
    lane_hot,
    spread,
    own_part,
    rad_part,
    rad_ssem,
    rad_rsem,
    hal_ssem,
    hal_rsem,
    side_ssem,
    side_rsem,
    piece_ssem,
    piece_rsem,
    val_ssem,
    val_rsem,
):
    fields, rows, columns = c_ref.shape
    slots = key_ref.shape[1]
    per_tile = columns // tiles
    nblk = columns // BLK
    panel = lax.axis_index("panel")
    rad = lax.axis_index("rad")
    hor = lax.axis_index("hor")
    other = 1 - panel

    barrier = pltpu.get_barrier_semaphore()

    def greet(j, carry):
        pl.semaphore_signal(
            barrier, inc=1, device_id={"panel": other, "hor": j}, device_id_type=MESH
        )
        return carry

    lax.fori_loop(0, tiles, greet, 0)

    has_low, has_high = rad > 0, rad < levels - 1
    has_north, has_south = hor > 0, hor < tiles - 1

    def to_rad(step):
        return {"rad": rad + step}

    def to_hor(step):
        return {"hor": hor + step}

    around = (
        (has_low, to_rad(-1)),
        (has_high, to_rad(1)),
        (has_north, to_hor(-1)),
        (has_south, to_hor(1)),
    )
    for present, where in around:

        @pl.when(present)
        def _():
            pl.semaphore_signal(barrier, inc=1, device_id=where, device_id_type=MESH)

    row_ids = lax.broadcasted_iota(jnp.int32, (rows, BLK), 0)
    lane_ids = lax.broadcasted_iota(jnp.int32, (rows, BLK), 1)
    bad_row = ((row_ids == 0) & (hor == 0)) | ((row_ids == rows - 1) & (hor == tiles - 1))

    def border_mask(block):
        col = lane_ids + block * BLK
        return bad_row | (col == 0) | (col == columns - 1)

    def rad_copy(ph, src, up):
        slot = 0 if up else 1
        return pltpu.make_async_remote_copy(
            src_ref=src,
            dst_ref=rad_buf.at[ph, slot],
            send_sem=rad_ssem.at[ph, slot],
            recv_sem=rad_rsem.at[ph, slot],
            device_id=to_rad(1 if up else -1),
            device_id_type=MESH,
        )

    def val_copy(ph, up):
        slot = 0 if up else 1
        return pltpu.make_async_remote_copy(
            src_ref=val_send.at[ph],
            dst_ref=val_recv.at[ph, slot],
            send_sem=val_ssem.at[ph, slot],
            recv_sem=val_rsem.at[ph, slot],
            device_id=to_rad(1 if up else -1),
            device_id_type=MESH,
        )

    def hal_copy(ph, down):
        slot = 0 if down else 1
        return pltpu.make_async_remote_copy(
            src_ref=hal_send.at[ph, slot],
            dst_ref=hal_recv.at[ph, slot],
            send_sem=hal_ssem.at[ph, slot],
            recv_sem=hal_rsem.at[ph, slot],
            device_id=to_hor(1 if down else -1),
            device_id_type=MESH,
        )

    def side_copy(ph, j):
        return pltpu.make_async_remote_copy(
            src_ref=side_msg.at[ph],
            dst_ref=side_buf.at[ph, hor],
            send_sem=side_ssem.at[ph],
            recv_sem=side_rsem.at[ph],
            device_id={"panel": other, "hor": j},
            device_id_type=MESH,
        )

    def sides_all(ph):
        return pltpu.make_async_remote_copy(
            src_ref=side_buf.at[ph],
            dst_ref=side_buf.at[ph],
            send_sem=side_ssem.at[ph],
            recv_sem=side_rsem.at[ph],
            device_id={"panel": other},
            device_id_type=MESH,
        )

    def piece_copy(ph, edge, j):
        return pltpu.make_async_remote_copy(
            src_ref=pieces.at[ph, j],
            dst_ref=row_buf.at[ph, edge],
            send_sem=piece_ssem.at[ph],
            recv_sem=piece_rsem.at[ph, edge],
            device_id={"panel": other, "hor": j},
            device_id_type=MESH,
        )

    def pieces_all(ph):
        return pltpu.make_async_remote_copy(
            src_ref=pieces.at[ph],
            dst_ref=pieces.at[ph],
            send_sem=piece_ssem.at[ph],
            recv_sem=piece_rsem.at[ph, 0],
            device_id={"panel": other},
            device_id_type=MESH,
        )

    def pack_border(ph, src):
        lanes = lax.broadcasted_iota(jnp.int32, (rows, 128), 1)
        both = jnp.zeros((rows, 128), F32)
        for f in range(fields):
            first = src[f, :, 0:1]
            last = src[f, :, columns - 1 : columns]
            both = jnp.where(lanes == f, first, both)
            both = jnp.where(lanes == fields + f, last, both)
        turned = pltpu.roll(both, 0, 1, stride=2 * fields, stride_axis=0)
        side_msg[ph] = jnp.sum(turned, axis=0, keepdims=True)

        for edge, row, here in ((0, 0, hor == 0), (1, rows - 1, hor == tiles - 1)):

            @pl.when(here)
            def _():
                for f in range(fields):
                    row_line[f : f + 1, 0:columns] = src[f, row : row + 1, :]
                row_line[:, columns : columns + 128] = jnp.zeros((fields, 128), F32)
                for j in range(tiles):
                    base, off = divmod(per_tile * j, 128)
                    one = row_line[:, base * 128 : base * 128 + 128]
                    if off:
                        two = row_line[:, base * 128 + 128 : base * 128 + 256]
                        one = pltpu.roll(one, 128 - off, 1)
                        two = pltpu.roll(two, 128 - off, 1)
                        one = jnp.where(lanes < 128 - off, one, two)
                    pieces[ph, j] = one

    def send_border(ph):
        def one(j, carry):
            side_copy(ph, j).start()
            return carry

        lax.fori_loop(0, tiles, one, 0)
        for edge, here in ((0, hor == 0), (1, hor == tiles - 1)):

            @pl.when(here)
            def _():
                def row(j, carry):
                    piece_copy(ph, edge, j).start()
                    return carry

                lax.fori_loop(0, tiles, row, 0)

    def send_rad(ph, src):
        @pl.when(has_high)
        def _():
            rad_copy(ph, src, True).start()

        @pl.when(has_low)
        def _():
            rad_copy(ph, src, False).start()

    def prepare():
        tgt = tgt_ref[0]
        don = don_ref[0]
        slot_ids = lax.broadcasted_iota(jnp.int32, (1, slots), 1)
        live_ref[...] = jnp.where(slot_ids < cnt_ref[...], wt_ref[0], F32(0.0))
        first = tgt - per_tile * hor
        second = tgt - columns - per_tile * hor
        entry = jnp.where(
            tgt < columns, first, jnp.where(tgt < 2 * columns, second + 128, -1)
        )
        ids = lax.broadcasted_iota(jnp.int32, (BLK, slots), 0)
        gather_rows[...] = jnp.where(ids == entry, F32(1), F32(0)).astype(BF16)
        place = tgt - 2 * columns
        far = jnp.where(place >= tiles * rows, 1, 0)
        line = place - far * (tiles * rows)
        tile = jnp.where(place >= 0, line >> 3, -1)
        hids = lax.broadcasted_iota(jnp.int32, (tiles, slots), 0)
        gather_sides[...] = jnp.where(hids == tile, F32(1), F32(0)).astype(BF16)
        side_group[...] = 2 * (line & 7) + far
        local = jnp.zeros_like(don)
        for m in range(1, rows):
            local = local + jnp.where(don >= m * columns, 1, 0)
        col = don - local * columns
        key_ref[...] = (col >> 8) * rows + local
        hot = jnp.where(ids == (col & (BLK - 1)), F32(1), F32(0)).astype(BF16)
        lane_hot[:, 0:slots] = hot
        lane_hot[:, slots : 2 * slots] = hot

    def gather(ph):
        table = jnp.concatenate([row_buf[ph, 0], row_buf[ph, 1]], axis=1)
        hi, lo = split(table)
        got = jnp.dot(
            jnp.concatenate([hi, lo], axis=0), gather_rows[...], preferred_element_type=F32
        )
        from_rows = got[0:fields] + got[fields : 2 * fields]
        turned = side_buf[ph, :, 0, :].T
        hi, lo = split(turned)
        got = jnp.dot(
            jnp.concatenate([hi, lo], axis=0), gather_sides[...], preferred_element_type=F32
        )
        got = got[0:128] + got[128:256]
        total = from_rows
        group = side_group[...]
        for g in range(2 * rows):
            part = got[g * fields : (g + 1) * fields]
            total = total + jnp.where(group == g, part, F32(0.0))
        return total * live_ref[...]

    def scatter(values, into):
        hi, lo = split(values)
        hi, lo = hi.astype(F32), lo.astype(F32)
        key = key_ref[...]
        own = lax.broadcasted_iota(jnp.int32, (rows, slots), 0)

        def one(block, carry):
            hit = key == own + block * rows
            at = pl.multiple_of(block * (fields * rows), fields * rows)
            for part, x in ((0, hi), (1, lo)):
                picked = [jnp.where(hit, x[f : f + 1], F32(0.0)) for f in range(fields)]
                spread[pl.ds(at, fields * rows), part * slots : (part + 1) * slots] = (
                    jnp.concatenate(picked, axis=0).astype(BF16)
                )
            return carry

        lax.fori_loop(0, nblk, one, 0)
        into[...] = lax.dot_general(
            spread[...], lane_hot[...], (((1,), (1,)), ((), ())), preferred_element_type=F32
        )

    def coefficients(f):
        low = rs_ref[1, f, jnp.maximum(rad - 1, 0)]
        high = rs_ref[2, f, jnp.minimum(rad + 1, levels - 1)]
        low = jnp.where(has_low, low, F32(0.0))
        high = jnp.where(has_high, high, F32(0.0))
        return low, high

    def overset(ph, src):
        sides_all(ph).wait_recv()
        piece_copy(ph, 0, 0).wait_recv()
        piece_copy(ph, 1, 0).wait_recv()
        values = gather(ph)
        val_send[ph] = values

        @pl.when(has_high)
        def _():
            val_copy(ph, True).start()

        @pl.when(has_low)
        def _():
            val_copy(ph, False).start()

        scatter(values, own_part)

        def one(block, carry):
            at = pl.multiple_of(block * BLK, BLK)
            border = border_mask(block)
            for f in range(fields):
                start = pl.multiple_of(block * (fields * rows) + f * rows, rows)
                x = jnp.where(border, F32(0.0), src[f, :, pl.ds(at, BLK)])
                x = x + own_part[pl.ds(start, rows), :]
                v_ref[ph, f, :, pl.ds(at + 128, BLK)] = x
                hal_send[ph, 0, f : f + 1, pl.ds(at, BLK)] = x[rows - 1 : rows]
                hal_send[ph, 1, f : f + 1, pl.ds(at, BLK)] = x[0:1]
            return carry

        lax.fori_loop(0, nblk, one, 0)

        @pl.when(has_south)
        def _():
            hal_copy(ph, True).start()

        @pl.when(has_north)
        def _():
            hal_copy(ph, False).start()

        @pl.when(has_low)
        def _():
            val_copy(ph, True).wait_recv()

        @pl.when(has_high)
        def _():
            val_copy(ph, False).wait_recv()

        mixed = []
        for f in range(fields):
            low, high = coefficients(f)
            mixed.append(
                low * val_recv[ph, 0, f : f + 1, :] + high * val_recv[ph, 1, f : f + 1, :]
            )
        scatter(jnp.concatenate(mixed, axis=0), rad_part)

    def wait_neighbours(ph, src):
        @pl.when(has_low)
        def _():
            rad_copy(ph, src, True).wait_recv()

        @pl.when(has_high)
        def _():
            rad_copy(ph, src, False).wait_recv()

        @pl.when(has_north)
        def _():
            hal_copy(ph, True).wait_recv()

        @pl.when(has_south)
        def _():
            hal_copy(ph, False).wait_recv()

    def wait_sends(ph, src):
        for present, copy in (
            (has_high, lambda: rad_copy(ph, src, True)),
            (has_low, lambda: rad_copy(ph, src, False)),
            (has_high, lambda: val_copy(ph, True)),
            (has_low, lambda: val_copy(ph, False)),
            (has_south, lambda: hal_copy(ph, True)),
            (has_north, lambda: hal_copy(ph, False)),
            ((hor == 0) | (hor == tiles - 1), lambda: pieces_all(ph)),
        ):

            @pl.when(present)
            def _():
                copy().wait_send()

        sides_all(ph).wait_send()

    def operator(ph, finish):
        def one(block, carry):
            at = pl.multiple_of(block * BLK, BLK)
            cols = pl.ds(at, BLK)
            kap = kap_ref[0, 0, :, cols]
            vt = vt_ref[0, 0, :, cols]
            vp = vp_ref[0, 0, :, cols]
            north, south = kap + vt, kap - vt
            east, west = kap + vp, kap - vp
            center = 4.0 * kap
            border = border_mask(block)
            here, total = [], []
            for f in range(fields):
                wide = v_ref[ph, f, :, pl.ds(at, BLK + 256)]
                cur = wide[:, 128 : 128 + BLK]
                before = pltpu.roll(wide, 1, 1)[:, 128 : 128 + BLK]
                after = pltpu.roll(wide, BLK + 255, 1)[:, 128 : 128 + BLK]
                below = jnp.where(
                    row_ids == 0, hal_recv[ph, 0, f : f + 1, cols], pltpu.roll(cur, 1, 0)
                )
                above = jnp.where(
                    row_ids == rows - 1,
                    hal_recv[ph, 1, f : f + 1, cols],
                    pltpu.roll(cur, rows - 1, 0),
                )
                low, high = coefficients(f)
                start = pl.multiple_of(block * (fields * rows) + f * rows, rows)
                mixed = low * rad_buf[ph, 0, f, :, cols] + high * rad_buf[ph, 1, f, :, cols]
                acc = jnp.where(border, F32(0.0), mixed) + rad_part[pl.ds(start, rows), :]
                acc = acc + south * below + north * above + west * before + east * after
                acc = acc - center * cur + rs_ref[0, f, rad] * cur
                here.append(cur)
                total.append(acc)
            for e in range(fields):
                acc = total[e]
                for f in range(fields):
                    acc = acc + fc_ref[rad, f, e] * here[f]
                finish(e, cols, at, here[e], acc)
            return carry

        lax.fori_loop(0, nblk, one, 0)

    pack_border(0, c_ref)
    zero_block = jnp.zeros((2, fields, rows, 128), F32)
    v_ref[:, :, :, 0:128] = zero_block
    v_ref[:, :, :, columns + 128 : columns + 256] = zero_block
    for present, slot in ((has_low, 0), (has_high, 1)):

        @pl.when(jnp.logical_not(present))
        def _():
            for ph in range(2):
                rad_buf[ph, slot] = jnp.zeros(rad_buf.shape[2:], F32)
                val_recv[ph, slot] = jnp.zeros(val_recv.shape[2:], F32)

    for present, slot in ((has_north, 0), (has_south, 1)):

        @pl.when(jnp.logical_not(present))
        def _():
            for ph in range(2):
                hal_recv[ph, slot] = jnp.zeros(hal_recv.shape[2:], F32)

    count = tiles
    for present, _ in around:
        count = count + jnp.where(present, 1, 0)
    pl.semaphore_wait(barrier, count)

    send_rad(0, c_ref)
    send_border(0)
    prepare()
    overset(0, c_ref)
    wait_neighbours(0, c_ref)

    def pulled(e, cols, at, here, acc):
        w_ref[e, :, cols] = STEP_SIZE * acc

    operator(0, pulled)

    send_rad(1, w_ref)
    pack_border(1, w_ref)
    send_border(1)
    overset(1, w_ref)
    wait_neighbours(1, w_ref)

    def final(e, cols, at, here, acc):
        out_ref[e, :, cols] = (
            v_ref[0, e, :, pl.ds(at + 128, BLK)] + here + (0.5 * STEP_SIZE) * acc
        )

    operator(1, final)
    wait_sends(0, c_ref)
    wait_sends(1, w_ref)


def body(
    final_cotangent,
    diffusivity,
    theta_velocity,
    phi_velocity,
    radial_stencil,
    field_coupling,
    slot_targets,
    slot_donors,
    slot_weights,
    slot_counts,
):
    fields, _, rows, columns = final_cotangent.shape[1:]
    tiles, levels = lax.axis_size("hor"), lax.axis_size("rad")
    slots = slot_targets.shape[-1]
    nblk = columns // BLK
    block = (fields, rows, columns)
    vmem = pl.BlockSpec(memory_space=pltpu.VMEM)
    smem = pl.BlockSpec(memory_space=pltpu.SMEM)
    dma = pltpu.SemaphoreType.DMA
    out = pl.pallas_call(
        functools.partial(kernel, tiles, levels),
        out_shape=jax.ShapeDtypeStruct(block, F32),
        in_specs=[vmem, vmem, vmem, vmem, smem, smem, vmem, vmem, vmem, vmem],
        out_specs=vmem,
        scratch_shapes=[
            pltpu.VMEM(block, F32),
            pltpu.VMEM((2, fields, rows, columns + 256), F32),
            pltpu.VMEM((2, 2, *block), F32),
            pltpu.VMEM((2, 2, fields, columns), F32),
            pltpu.VMEM((2, 2, fields, columns), F32),
            pltpu.VMEM((2, 1, 128), F32),
            pltpu.VMEM((2, tiles, 1, 128), F32),
            pltpu.VMEM((fields, columns + 128), F32),
            pltpu.VMEM((2, tiles, fields, 128), F32),
            pltpu.VMEM((2, 2, fields, 128), F32),
            pltpu.VMEM((2, fields, slots), F32),
            pltpu.VMEM((2, 2, fields, slots), F32),
            pltpu.VMEM((BLK, slots), BF16),
            pltpu.VMEM((tiles, slots), BF16),
            pltpu.VMEM((1, slots), jnp.int32),
            pltpu.VMEM((1, slots), jnp.int32),
            pltpu.VMEM((1, slots), F32),
            pltpu.VMEM((BLK, 2 * slots), BF16),
            pltpu.VMEM((nblk * fields * rows, 2 * slots), BF16),
            pltpu.VMEM((nblk * fields * rows, BLK), F32),
            pltpu.VMEM((nblk * fields * rows, BLK), F32),
            dma((2, 2)),
            dma((2, 2)),
            dma((2, 2)),
            dma((2, 2)),
            dma((2,)),
            dma((2,)),
            dma((2,)),
            dma((2, 2)),
            dma((2, 2)),
            dma((2, 2)),
        ],
        compiler_params=pltpu.CompilerParams(
            collective_id=0, has_side_effects=True, vmem_limit_bytes=40 * 2**20
        ),
        cost_estimate=pl.CostEstimate(
            flops=8_000_000, bytes_accessed=1_500_000, transcendentals=0
        ),
    )(
        final_cotangent.reshape(block),
        diffusivity,
        theta_velocity,
        phi_velocity,
        radial_stencil,
        field_coupling,
        slot_targets,
        slot_donors,
        slot_weights,
        slot_counts,
    )
    return out.reshape(final_cotangent.shape)


def solution(mesh):
    return jax.shard_map(
        body,
        mesh=mesh,
        in_specs=(
            P("panel", None, "rad", "hor", None),
            P("panel", "rad", "hor", None),
            P("panel", "rad", "hor", None),
            P("panel", "rad", "hor", None),
            P(),
            P(),
            P("panel", "hor", None),
            P("panel", "hor", None),
            P("panel", "hor", None),
            P("panel", "hor"),
        ),
        out_specs=P("panel", None, "rad", "hor", None),
        check_vma=False,
    )
```

time: 236 us -> 86.1 us (0.36)
  Pallas kernels: 0 us -> 77.6 us
  starting transfers between devices: 49.5 us -> 0 us
  other arithmetic: 49 us -> 0 us
  waiting for transfers between devices: 43.4 us -> 0 us
  blocking collectives: 40 us -> 0 us
  local copies, waits for them, and re-layouts: 29.9 us -> 6.69 us
  matrix products: 21.7 us -> 0 us
    pallas_call x0 -> x1, Pallas kernels: none -> 77.6 us  [body(): pl.pallas_call(functools.partial(kernel, tiles, levels), out_shape=jax.Sh...]
    all_to_all x2 -> x0, blocking collectives: 40 us -> none  [the longest x1 23.7 us: summed_on_arrival(): lax.all_to_all(parts, axis, split_axis=0, concat_axis=0, tiled=True)]
    scatter-add x2 -> x0, other arithmetic: 34 us -> none  [transpose_overset(): return kept.at[:, donor_index].add(values).reshape(cotangent.shape)]
    ppermute x12 -> x0, waiting for transfers between devices: 30.6 us -> none  [the longest x4 18.4 us: extended(): lax.ppermute(last, axis, up)]
    all_to_all x2 -> x0, starting transfers between devices: 26.3 us -> none  [the longest x1 14.1 us: summed_on_arrival(): lax.all_to_all(parts, axis, split_axis=0, concat_axis=0, tiled=True)]
    ppermute x12 -> x0, starting transfers between devices: 23.2 us -> none  [the longest x4 14.1 us: extended(): lax.ppermute(last, axis, up)]
    dot_general x2 -> x0, matrix products: 21.7 us -> none  [transpose_operator(): jnp.einsum('rfe,frij->erij', coupling_here, cotangent, precision=lax.Prec...]
    reshape x7 -> x0, local copies, waits for them, and re-layouts: 16.4 us -> none  [the longest x2 11 us: transpose_overset(): return kept.at[:, donor_index].add(values).reshape(cotangent.shape)]
  transfers between devices with their start and end apart: 14 -> 0, of which waited for: 6 -> 0; matrix products, arithmetic and copies ran while one was open for 11% -> 0% of each run, Pallas kernels for 0% -> 0%
where the time goes in v1:
time: 86.1 us; the launch traced here: 85 us
  Pallas kernels  77.6 us (90%)
  local copies, waits for them, and re-layouts  6.69 us (8%)
    pallas_call x1, Pallas kernels, body(): pl.pallas_call(functools.partial(kernel, tiles, levels), out_shape=jax.Sh...  77.6 us
    unnamed x18, local copies, waits for them, and re-layouts  6.69 us

profile of v1, /device:TPU:32, one launch (start us, length us, event | category | flops | bytes accessed | tf_op | source)
XLA Modules:
  0.0 85.0 jit_solution(4216274631355971059)
XLA Ops:
  0.0 0.0 copy-start.4
  0.7 0.0 copy-start.5
  0.7 0.8 copy.11.rs_ref
  1.5 0.0 copy-done.4
  1.5 0.0 copy-done.5
  1.5 0.0 copy-start
  1.5 1.1 %copy-done = f32[1,8,1,8,2304]{4,3,2,1,0:T(8,128)S(1)} copy-done((f32[1,8,1,8,2304]{4,3,2,1,0:T(8,128)S(1)}, f32[1,8,1,8,2304]{4,3,2,1,0:T(8,128)}, u32[]{:S(2)}) %copy-start) | copy-done | bytes 589848
  2.5 0.0 copy-start.1
  2.5 0.9 %copy-done.1 = f32[1,1,8,2304]{3,2,1,0:T(8,128)S(1)} copy-done((f32[1,1,8,2304]{3,2,1,0:T(8,128)S(1)}, f32[1,1,8,2304]{3,2,1,0:T(8,128)}, u32[]{:S(2)}) %copy-start.1) | copy-done | bytes 73752
  3.4 0.0 copy-start.2
  3.4 0.9 %copy-done.2 = f32[1,1,8,2304]{3,2,1,0:T(8,128)S(1)} copy-done((f32[1,1,8,2304]{3,2,1,0:T(8,128)S(1)}, f32[1,1,8,2304]{3,2,1,0:T(8,128)}, u32[]{:S(2)}) %copy-start.2) | copy-done | bytes 73752
  4.3 0.0 copy-start.3
  4.3 0.9 %copy-done.3 = f32[1,1,8,2304]{3,2,1,0:T(8,128)S(1)} copy-done((f32[1,1,8,2304]{3,2,1,0:T(8,128)S(1)}, f32[1,1,8,2304]{3,2,1,0:T(8,128)}, u32[]{:S(2)}) %copy-start.3) | copy-done | bytes 73752
  5.2 0.0 copy-start.6
  5.2 0.7 copy-done.6
  5.9 0.0 copy-start.7
  5.9 0.7 copy-done.7
  6.6 77.6 %shard_map.100 = f32[8,8,2304]{2,1,0:T(8,128)S(1)} custom-call(f32[8,8,2304]{2,1,0:T(8,128)S(1)} %bitcast.5, f32[1,1,8,2304]{3,2,1,0:T(8,128)S(1)} %copy-done.1, f32[1,1,8,2304]{3,2,1,0:T(8,128)S(1)} %copy-done.2, f32[1,1,8,2304]{3,2,1,0:T(8,128)S(1)} %copy-done.3, f32[3,8,4]{2,1,0:T(8,128)S(1)} %copy.11.rs_ref, f32[4,8,8]{2,1,0:T(8,128)S(1)} %copy-done.4, ...), custom_call_target="tpu_custom_call" | custom-call | flops 8000000 | bytes 1500000 | tf_op jit(solution)/shard_map/pallas_call | solution.py:521
  84.2 0.8 copy.15
Async XLA Ops:
  0.0 1.5 %copy-start.4 = (f32[4,8,8]{2,1,0:T(8,128)S(1)}, f32[4,8,8]{2,1,0:T(8,128)}, u32[]{:S(2)}) copy-start(f32[4,8,8]{2,1,0:T(8,128)} %fc_ref.1) | copy-start | bytes 3076
  0.7 0.8 copy-start.5
  1.5 1.1 %copy-start = (f32[1,8,1,8,2304]{4,3,2,1,0:T(8,128)S(1)}, f32[1,8,1,8,2304]{4,3,2,1,0:T(8,128)}, u32[]{:S(2)}) copy-start(f32[1,8,1,8,2304]{4,3,2,1,0:T(8,128)} %param.10) | copy-start | bytes 1769476
  2.5 0.9 %copy-start.1 = (f32[1,1,8,2304]{3,2,1,0:T(8,128)S(1)}, f32[1,1,8,2304]{3,2,1,0:T(8,128)}, u32[]{:S(2)}) copy-start(f32[1,1,8,2304]{3,2,1,0:T(8,128)} %kap_ref.1) | copy-start | bytes 221188
  3.4 0.9 %copy-start.2 = (f32[1,1,8,2304]{3,2,1,0:T(8,128)S(1)}, f32[1,1,8,2304]{3,2,1,0:T(8,128)}, u32[]{:S(2)}) copy-start(f32[1,1,8,2304]{3,2,1,0:T(8,128)} %vt_ref.1) | copy-start | bytes 221188
  4.3 0.9 %copy-start.3 = (f32[1,1,8,2304]{3,2,1,0:T(8,128)S(1)}, f32[1,1,8,2304]{3,2,1,0:T(8,128)}, u32[]{:S(2)}) copy-start(f32[1,1,8,2304]{3,2,1,0:T(8,128)} %vp_ref.1) | copy-start | bytes 221188
  5.2 0.7 copy-start.6
  5.9 0.7 copy-start.7

commit v2 on v1

v2 whole, which is shorter than its diff:
```python
import functools

import jax
import jax.numpy as jnp
from jax import lax
from jax.experimental import pallas as pl
from jax.experimental.pallas import tpu as pltpu
from jax.sharding import PartitionSpec as P

STEP_SIZE = 0.2
MESH = pl.DeviceIdType.MESH
F32 = jnp.float32
BF16 = jnp.bfloat16
BLK = 256


def split(x):
    hi = x.astype(BF16)
    lo = (x - hi.astype(F32)).astype(BF16)
    return hi, lo


def kernel(
    tiles,
    levels,
    chunks,
    c_hbm,
    kap_hbm,
    vt_hbm,
    vp_hbm,
    rs_ref,
    fc_ref,
    tgt_hbm,
    don_hbm,
    wt_hbm,
    cnt_ref,
    out_ref,
    c_ref,
    coef,
    ints,
    wts,
    w_ref,
    v_ref,
    rad_buf,
    hal_send,
    hal_recv,
    side_msg,
    side_buf,
    row_line,
    pieces,
    row_buf,
    val_send,
    val_recv,
    info,
    gather_rows,
    gather_sides,
    side_group,
    key_ref,
    lane_hot,
    spread,
    own_part,
    rad_part,
    hal_part,
    load_sem,
    rad_ssem,
    rad_rsem,
    hal_ssem,
    hal_rsem,
    side_ssem,
    side_rsem,
    piece_ssem,
    piece_rsem,
    val_ssem,
    val_rsem,
    info_ssem,
    info_rsem,
):
    fields, rows, columns = c_ref.shape
    slots = key_ref.shape[2]
    window = row_buf.shape[3]
    per_tile = columns // tiles
    nblk = columns // BLK
    width = columns // chunks
    panel = lax.axis_index("panel")
    rad = lax.axis_index("rad")
    hor = lax.axis_index("hor")
    other = 1 - panel

    barrier = pltpu.get_barrier_semaphore()

    def greet(j, carry):
        pl.semaphore_signal(
            barrier, inc=1, device_id={"panel": other, "hor": j}, device_id_type=MESH
        )
        return carry

    lax.fori_loop(0, tiles, greet, 0)

    has_low, has_high = rad > 0, rad < levels - 1
    has_north, has_south = hor > 0, hor < tiles - 1

    def to_rad(step):
        return {"rad": rad + step}

    def to_hor(step):
        return {"hor": hor + step}

    around = (
        (has_low, to_rad(-1)),
        (has_high, to_rad(1)),
        (has_north, to_hor(-1)),
        (has_south, to_hor(1)),
    )
    for present, where in around:

        @pl.when(present)
        def _():
            pl.semaphore_signal(barrier, inc=1, device_id=where, device_id_type=MESH)

    loads = [
        pltpu.make_async_copy(src, dst, load_sem.at[k])
        for k, (src, dst) in enumerate(
            (
                (c_hbm, c_ref),
                (kap_hbm.at[0, 0], coef.at[0]),
                (vt_hbm.at[0, 0], coef.at[1]),
                (vp_hbm.at[0, 0], coef.at[2]),
                (tgt_hbm, ints.at[0]),
                (don_hbm, ints.at[1]),
                (wt_hbm, wts),
            )
        )
    ]
    for load in loads:
        load.start()

    row_ids = lax.broadcasted_iota(jnp.int32, (rows, BLK), 0)
    lane_ids = lax.broadcasted_iota(jnp.int32, (rows, BLK), 1)
    bad_row = ((row_ids == 0) & (hor == 0)) | ((row_ids == rows - 1) & (hor == tiles - 1))

    def side_mask(block):
        col = lane_ids + block * BLK
        return (col == 0) | (col == columns - 1)

    def remote(src, dst, send, recv, where):
        return pltpu.make_async_remote_copy(
            src_ref=src,
            dst_ref=dst,
            send_sem=send,
            recv_sem=recv,
            device_id=where,
            device_id_type=MESH,
        )

    def rad_copy(ph, src, up, k):
        slot = 0 if up else 1
        cols = pl.ds(k * width, width)
        return remote(
            src.at[:, :, cols],
            rad_buf.at[ph, slot, :, :, cols],
            rad_ssem.at[ph, slot, k],
            rad_rsem.at[ph, slot, k],
            to_rad(1 if up else -1),
        )

    def hal_copy(ph, down, k):
        slot = 0 if down else 1
        cols = pl.ds(k * width, width)
        return remote(
            hal_send.at[ph, slot, :, cols],
            hal_recv.at[ph, slot, :, cols],
            hal_ssem.at[ph, slot, k],
            hal_rsem.at[ph, slot, k],
            to_hor(1 if down else -1),
        )

    def val_copy(ph, up):
        slot = 0 if up else 1
        return remote(
            val_send.at[ph],
            val_recv.at[ph, slot],
            val_ssem.at[ph, slot],
            val_rsem.at[ph, slot],
            to_rad(1 if up else -1),
        )

    def info_copy(down):
        slot = 0 if down else 1
        return remote(
            info.at[0],
            info.at[1 + slot],
            info_ssem.at[slot],
            info_rsem.at[slot],
            to_hor(1 if down else -1),
        )

    def side_copy(ph, j):
        return remote(
            side_msg.at[ph],
            side_buf.at[ph, hor],
            side_ssem.at[ph],
            side_rsem.at[ph],
            {"panel": other, "hor": j},
        )

    def sides_all(ph):
        return remote(
            side_buf.at[ph], side_buf.at[ph], side_ssem.at[ph], side_rsem.at[ph], {"panel": other}
        )

    def piece_copy(ph, edge, j):
        return remote(
            pieces.at[ph, j],
            row_buf.at[ph, edge],
            piece_ssem.at[ph],
            piece_rsem.at[ph, edge],
            {"panel": other, "hor": j},
        )

    def pieces_all(ph):
        return remote(
            pieces.at[ph], pieces.at[ph], piece_ssem.at[ph], piece_rsem.at[ph, 0], {"panel": other}
        )

    def pack_border(ph, src):
        lanes = lax.broadcasted_iota(jnp.int32, (rows, 128), 1)
        both = jnp.zeros((rows, 128), F32)
        for f in range(fields):
            first = src[f, :, 0:1]
            last = src[f, :, columns - 1 : columns]
            both = jnp.where(lanes == f, first, both)
            both = jnp.where(lanes == fields + f, last, both)
        turned = pltpu.roll(both, 0, 1, stride=2 * fields, stride_axis=0)
        side_msg[ph] = jnp.sum(turned, axis=0, keepdims=True)

        for edge, row, here in ((0, 0, hor == 0), (1, rows - 1, hor == tiles - 1)):

            @pl.when(here)
            def _():
                for f in range(fields):
                    row_line[f : f + 1, 128 : 128 + columns] = src[f, row : row + 1, :]
                row_line[:, 0:128] = jnp.zeros((fields, 128), F32)
                row_line[:, columns + 128 : columns + 384] = jnp.zeros((fields, 256), F32)
                for j in range(tiles):
                    base, off = divmod(128 + per_tile * (j - 1), 128)
                    one = row_line[:, base * 128 : base * 128 + window + 128]
                    if off:
                        one = pltpu.roll(one, window + 128 - off, 1)
                    pieces[ph, j] = one[:, 0:window]

    def send_border(ph):
        for edge, here in ((0, hor == 0), (1, hor == tiles - 1)):

            @pl.when(here)
            def _():
                def row(j, carry):
                    piece_copy(ph, edge, j).start()
                    return carry

                lax.fori_loop(0, tiles, row, 0)

        def one(j, carry):
            side_copy(ph, j).start()
            return carry

        lax.fori_loop(0, tiles, one, 0)

    def send_chunk(ph, src, k):
        for present, copy in (
            (has_high, lambda: rad_copy(ph, src, True, k)),
            (has_low, lambda: rad_copy(ph, src, False, k)),
            (has_south, lambda: hal_copy(ph, True, k)),
            (has_north, lambda: hal_copy(ph, False, k)),
        ):

            @pl.when(present)
            def _():
                copy().start()

    def wait_chunk(ph, src, k):
        for present, copy in (
            (has_low, lambda: rad_copy(ph, src, True, k)),
            (has_high, lambda: rad_copy(ph, src, False, k)),
            (has_north, lambda: hal_copy(ph, True, k)),
            (has_south, lambda: hal_copy(ph, False, k)),
        ):

            @pl.when(present)
            def _():
                copy().wait_recv()

    def prepare(which):
        tgt = info[which, 0].astype(jnp.int32)
        don = info[which, 1].astype(jnp.int32)
        at = pl.ds(which * slots, slots)
        first = tgt - per_tile * (hor - 1)
        second = first - columns + window
        entry = jnp.where(tgt < columns, first, jnp.where(tgt < 2 * columns, second, -1))
        ids = lax.broadcasted_iota(jnp.int32, (2 * window, slots), 0)
        gather_rows[:, at] = jnp.where(ids == entry, F32(1), F32(0)).astype(BF16)
        place = tgt - 2 * columns
        far = jnp.where(place >= tiles * rows, 1, 0)
        line = place - far * (tiles * rows)
        tile = jnp.where(place >= 0, line >> 3, -1)
        hids = lax.broadcasted_iota(jnp.int32, (tiles, slots), 0)
        gather_sides[:, at] = jnp.where(hids == tile, F32(1), F32(0)).astype(BF16)
        side_group[:, at] = 2 * (line & 7) + far
        local = jnp.zeros_like(don)
        for m in range(1, rows):
            local = local + jnp.where(don >= m * columns, 1, 0)
        col = don - local * columns
        block = col >> 8
        if which == 0:
            key_ref[which] = block * rows + local
        elif which == 1:
            key_ref[which] = jnp.where(local == rows - 1, block, -1)
        else:
            key_ref[which] = jnp.where(local == 0, block, -1)
        lane = jnp.broadcast_to((col & (BLK - 1)).astype(F32), (8, slots)).T[:, 0:1]
        ids = lax.broadcasted_iota(jnp.int32, (slots, BLK), 1).astype(F32)
        hot = jnp.where(ids == lane, F32(1), F32(0)).astype(BF16)
        lane_hot[which, 0:slots, :] = hot
        lane_hot[which, slots : 2 * slots, :] = hot

    def gather(ph):
        table = jnp.concatenate([row_buf[ph, 0], row_buf[ph, 1]], axis=1)
        hi, lo = split(table)
        got = jnp.dot(
            jnp.concatenate([hi, lo], axis=0), gather_rows[...], preferred_element_type=F32
        )
        total = got[0:fields] + got[fields : 2 * fields]
        turned = side_buf[ph, :, 0, :].T
        hi, lo = split(turned)
        got = jnp.dot(
            jnp.concatenate([hi, lo], axis=0), gather_sides[...], preferred_element_type=F32
        )
        got = got[0:128] + got[128:256]
        group = side_group[...]
        for g in range(2 * rows):
            part = got[g * fields : (g + 1) * fields]
            total = total + jnp.where(group == g, part, F32(0.0))
        return [
            total[:, n * slots : (n + 1) * slots] * info[n, 2] for n in range(3)
        ]

    def scatter(values, into):
        hi, lo = split(values)
        hi, lo = hi.astype(F32), lo.astype(F32)
        key = key_ref[0]
        own = lax.broadcasted_iota(jnp.int32, (rows, slots), 0)

        def one(block, carry):
            hit = key == own + block * rows
            at = pl.multiple_of(block * (fields * rows), fields * rows)
            for part, x in ((0, hi), (1, lo)):
                picked = [jnp.where(hit, x[f : f + 1], F32(0.0)) for f in range(fields)]
                spread[pl.ds(at, fields * rows), part * slots : (part + 1) * slots] = (
                    jnp.concatenate(picked, axis=0).astype(BF16)
                )
            return carry

        lax.fori_loop(0, nblk, one, 0)
        into[...] = jnp.dot(spread[...], lane_hot[0], preferred_element_type=F32)

    def scatter_row(which, values):
        hi, lo = split(values)
        key = key_ref[which]
        both = []
        for x in (hi.astype(F32), lo.astype(F32)):
            picked = [jnp.where(key == b, x, F32(0.0)) for b in range(nblk)]
            both.append(jnp.concatenate(picked, axis=0).astype(BF16))
        hal_part[which - 1] = jnp.dot(
            jnp.concatenate(both, axis=1), lane_hot[which], preferred_element_type=F32
        )

    def coefficients(f):
        low = rs_ref[1, f, jnp.maximum(rad - 1, 0)]
        high = rs_ref[2, f, jnp.minimum(rad + 1, levels - 1)]
        low = jnp.where(has_low, low, F32(0.0))
        high = jnp.where(has_high, high, F32(0.0))
        return low, high

    def overset(ph, src):
        sides_all(ph).wait_recv()
        piece_copy(ph, 0, 0).wait_recv()
        piece_copy(ph, 1, 0).wait_recv()
        values, from_north, from_south = gather(ph)
        val_send[ph] = values

        @pl.when(has_high)
        def _():
            val_copy(ph, True).start()

        @pl.when(has_low)
        def _():
            val_copy(ph, False).start()

        scatter(values, own_part)

        def one(block, carry):
            at = pl.multiple_of(block * BLK, BLK)
            border = bad_row | side_mask(block)
            for f in range(fields):
                start = pl.multiple_of(block * (fields * rows) + f * rows, rows)
                x = jnp.where(border, F32(0.0), src[f, :, pl.ds(at, BLK)])
                v_ref[ph, f, :, pl.ds(at + 128, BLK)] = x + own_part[pl.ds(start, rows), :]
            return carry

        lax.fori_loop(0, nblk, one, 0)
        scatter_row(1, from_north)
        scatter_row(2, from_south)

        @pl.when(has_low)
        def _():
            val_copy(ph, True).wait_recv()

        @pl.when(has_high)
        def _():
            val_copy(ph, False).wait_recv()

        mixed = []
        for f in range(fields):
            low, high = coefficients(f)
            mixed.append(
                low * val_recv[ph, 0, f : f + 1, :] + high * val_recv[ph, 1, f : f + 1, :]
            )
        scatter(jnp.concatenate(mixed, axis=0), rad_part)

    def wait_sends(ph, src):
        for k in range(chunks):
            for present, copy in (
                (has_high, lambda: rad_copy(ph, src, True, k)),
                (has_low, lambda: rad_copy(ph, src, False, k)),
                (has_south, lambda: hal_copy(ph, True, k)),
                (has_north, lambda: hal_copy(ph, False, k)),
            ):

                @pl.when(present)
                def _():
                    copy().wait_send()

        for present, copy in (
            (has_high, lambda: val_copy(ph, True)),
            (has_low, lambda: val_copy(ph, False)),
            ((hor == 0) | (hor == tiles - 1), lambda: pieces_all(ph)),
        ):

            @pl.when(present)
            def _():
                copy().wait_send()

        sides_all(ph).wait_send()

    def operator(ph, k, finish):
        def one(block, carry):
            at = pl.multiple_of(block * BLK, BLK)
            cols = pl.ds(at, BLK)
            kap = coef[0, :, cols]
            vt = coef[1, :, cols]
            vp = coef[2, :, cols]
            north, south = kap + vt, kap - vt
            east, west = kap + vp, kap - vp
            center = 4.0 * kap
            sides = side_mask(block)
            border = bad_row | sides
            here, total = [], []
            for f in range(fields):
                wide = v_ref[ph, f, :, pl.ds(at, BLK + 256)]
                cur = wide[:, 128 : 128 + BLK]
                before = pltpu.roll(wide, 1, 1)[:, 128 : 128 + BLK]
                after = pltpu.roll(wide, BLK + 255, 1)[:, 128 : 128 + BLK]
                line = block * fields + f
                edge = []
                for n in range(2):
                    raw = jnp.where(sides[0:1], F32(0.0), hal_recv[ph, n, f : f + 1, cols])
                    edge.append(raw + hal_part[n, pl.ds(line, 1), :])
                below = jnp.where(row_ids == 0, edge[0], pltpu.roll(cur, 1, 0))
                above = jnp.where(row_ids == rows - 1, edge[1], pltpu.roll(cur, rows - 1, 0))
                low, high = coefficients(f)
                start = pl.multiple_of(block * (fields * rows) + f * rows, rows)
                mixed = low * rad_buf[ph, 0, f, :, cols] + high * rad_buf[ph, 1, f, :, cols]
                acc = jnp.where(border, F32(0.0), mixed) + rad_part[pl.ds(start, rows), :]
                acc = acc + south * below + north * above + west * before + east * after
                acc = acc - center * cur + rs_ref[0, f, rad] * cur
                here.append(cur)
                total.append(acc)
            for e in range(fields):
                acc = total[e]
                for f in range(fields):
                    acc = acc + fc_ref[rad, f, e] * here[f]
                finish(e, cols, at, here[e], acc)
            return carry

        each = nblk // chunks
        lax.fori_loop(k * each, (k + 1) * each, one, 0)

    zero_block = jnp.zeros((2, fields, rows, 128), F32)
    v_ref[:, :, :, 0:128] = zero_block
    v_ref[:, :, :, columns + 128 : columns + 256] = zero_block
    for present, slot in ((has_low, 0), (has_high, 1)):

        @pl.when(jnp.logical_not(present))
        def _():
            for ph in range(2):
                rad_buf[ph, slot] = jnp.zeros(rad_buf.shape[2:], F32)
                val_recv[ph, slot] = jnp.zeros(val_recv.shape[2:], F32)

    for present, slot in ((has_north, 0), (has_south, 1)):

        @pl.when(jnp.logical_not(present))
        def _():
            info[1 + slot] = jnp.zeros(info.shape[1:], F32)
            for ph in range(2):
                hal_recv[ph, slot] = jnp.zeros(hal_recv.shape[2:], F32)

    for load in loads:
        load.wait()
    slot_ids = lax.broadcasted_iota(jnp.int32, (1, slots), 1)
    info[0, 0] = ints[0, 0].astype(F32)
    info[0, 1] = ints[1, 0].astype(F32)
    info[0, 2] = jnp.where(slot_ids < cnt_ref[0, 0], wts[0], F32(0.0))
    for f in range(fields):
        hal_send[0, 0, f : f + 1, :] = c_ref[f, rows - 1 : rows, :]
        hal_send[0, 1, f : f + 1, :] = c_ref[f, 0:1, :]
    pack_border(0, c_ref)

    count = tiles
    for present, _ in around:
        count = count + jnp.where(present, 1, 0)
    pl.semaphore_wait(barrier, count)

    for present, down in ((has_south, True), (has_north, False)):

        @pl.when(present)
        def _():
            info_copy(down).start()

    send_chunk(0, c_ref, 0)
    send_border(0)
    for k in range(1, chunks):
        send_chunk(0, c_ref, k)
    prepare(0)
    for present, down in ((has_north, True), (has_south, False)):

        @pl.when(present)
        def _():
            info_copy(down).wait_recv()

    prepare(1)
    prepare(2)
    overset(0, c_ref)

    def pulled(e, cols, at, here, acc):
        value = STEP_SIZE * acc
        w_ref[e, :, cols] = value
        hal_send[1, 0, e : e + 1, cols] = value[rows - 1 : rows]
        hal_send[1, 1, e : e + 1, cols] = value[0:1]

    for k in range(chunks):
        wait_chunk(0, c_ref, k)
        operator(0, k, pulled)
        if k == chunks - 1:
            pack_border(1, w_ref)
            send_border(1)
        send_chunk(1, w_ref, k)

    overset(1, w_ref)

    def final(e, cols, at, here, acc):
        out_ref[e, :, cols] = (
            v_ref[0, e, :, pl.ds(at + 128, BLK)] + here + (0.5 * STEP_SIZE) * acc
        )

    for k in range(chunks):
        wait_chunk(1, w_ref, k)
        operator(1, k, final)
    for present, down in ((has_south, True), (has_north, False)):

        @pl.when(present)
        def _():
            info_copy(down).wait_send()

    wait_sends(0, c_ref)
    wait_sends(1, w_ref)


def body(
    final_cotangent,
    diffusivity,
    theta_velocity,
    phi_velocity,
    radial_stencil,
    field_coupling,
    slot_targets,
    slot_donors,
    slot_weights,
    slot_counts,
):
    fields, _, rows, columns = final_cotangent.shape[1:]
    tiles, levels = lax.axis_size("hor"), lax.axis_size("rad")
    slots = slot_targets.shape[-1]
    nblk = columns // BLK
    chunks = 3 if nblk % 3 == 0 else 1
    window = -(-3 * (columns // tiles) // 128) * 128
    block = (fields, rows, columns)
    vmem = pl.BlockSpec(memory_space=pltpu.VMEM)
    smem = pl.BlockSpec(memory_space=pltpu.SMEM)
    hbm = pl.BlockSpec(memory_space=pltpu.HBM)
    dma = pltpu.SemaphoreType.DMA
    out = pl.pallas_call(
        functools.partial(kernel, tiles, levels, chunks),
        out_shape=jax.ShapeDtypeStruct(block, F32),
        in_specs=[hbm, hbm, hbm, hbm, smem, smem, hbm, hbm, hbm, smem],
        out_specs=vmem,
        scratch_shapes=[
            pltpu.VMEM(block, F32),
            pltpu.VMEM((3, rows, columns), F32),
            pltpu.VMEM((2, 1, 1, slots), jnp.int32),
            pltpu.VMEM((1, 1, slots), F32),
            pltpu.VMEM(block, F32),
            pltpu.VMEM((2, fields, rows, columns + 256), F32),
            pltpu.VMEM((2, 2, *block), F32),
            pltpu.VMEM((2, 2, fields, columns), F32),
            pltpu.VMEM((2, 2, fields, columns), F32),
            pltpu.VMEM((2, 1, 128), F32),
            pltpu.VMEM((2, tiles, 1, 128), F32),
            pltpu.VMEM((fields, columns + 384), F32),
            pltpu.VMEM((2, tiles, fields, window), F32),
            pltpu.VMEM((2, 2, fields, window), F32),
            pltpu.VMEM((2, fields, slots), F32),
            pltpu.VMEM((2, 2, fields, slots), F32),
            pltpu.VMEM((3, 3, 1, slots), F32),
            pltpu.VMEM((2 * window, 3 * slots), BF16),
            pltpu.VMEM((tiles, 3 * slots), BF16),
            pltpu.VMEM((1, 3 * slots), jnp.int32),
            pltpu.VMEM((3, 1, slots), jnp.int32),
            pltpu.VMEM((3, 2 * slots, BLK), BF16),
            pltpu.VMEM((nblk * fields * rows, 2 * slots), BF16),
            pltpu.VMEM((nblk * fields * rows, BLK), F32),
            pltpu.VMEM((nblk * fields * rows, BLK), F32),
            pltpu.VMEM((2, nblk * fields, BLK), F32),
            dma((7,)),
            dma((2, 2, chunks)),
            dma((2, 2, chunks)),
            dma((2, 2, chunks)),
            dma((2, 2, chunks)),
            dma((2,)),
            dma((2,)),
            dma((2,)),
            dma((2, 2)),
            dma((2, 2)),
            dma((2, 2)),
            dma((2,)),
            dma((2,)),
        ],
        compiler_params=pltpu.CompilerParams(
            collective_id=0, has_side_effects=True, vmem_limit_bytes=48 * 2**20
        ),
        cost_estimate=pl.CostEstimate(
            flops=8_000_000, bytes_accessed=1_500_000, transcendentals=0
        ),
    )(
        final_cotangent.reshape(block),
        diffusivity,
        theta_velocity,
        phi_velocity,
        radial_stencil,
        field_coupling,
        slot_targets,
        slot_donors,
        slot_weights,
        slot_counts,
    )
    return out.reshape(final_cotangent.shape)


def solution(mesh):
    return jax.shard_map(
        body,
        mesh=mesh,
        in_specs=(
            P("panel", None, "rad", "hor", None),
            P("panel", "rad", "hor", None),
            P("panel", "rad", "hor", None),
            P("panel", "rad", "hor", None),
            P(),
            P(),
            P("panel", "hor", None),
            P("panel", "hor", None),
            P("panel", "hor", None),
            P("panel", "hor"),
        ),
        out_specs=P("panel", None, "rad", "hor", None),
        check_vma=False,
    )
```

time: 86.1 us -> 75.2 us (0.87)
  the two profiles are of different devices: /device:TPU:32 before, /device:TPU:1 now
where the time goes in v2:
time: 75.2 us; the launch traced here: 74.9 us
  Pallas kernels  67.5 us (90%)
  local copies, waits for them, and re-layouts  6.69 us (9%)
    pallas_call x1, Pallas kernels, body(): pl.pallas_call(functools.partial(kernel, tiles, levels, chunks), out_shap...  67.5 us
    unnamed x18, local copies, waits for them, and re-layouts  6.69 us

profile of v2, /device:TPU:1, one launch (start us, length us, event | category | flops | bytes accessed | tf_op | source)
XLA Modules:
  0.0 74.9 jit_solution(13374345907584461468)
XLA Ops:
  0.0 0.0 copy-start.4
  0.7 0.0 copy-start.5
  0.7 0.8 %copy.11.rs_ref = f32[3,8,4]{2,1,0:T(8,128)S(1)} copy(f32[3,8,4]{1,2,0:T(4,128)} %param.14) | data formatting | bytes 768 | tf_op args[4]
  1.5 0.0 copy-done.4
  1.5 0.0 copy-done.5
  1.5 0.0 copy-start
  1.5 1.1 %copy-done = f32[1,8,1,8,2304]{4,3,2,1,0:T(8,128)S(1)} copy-done((f32[1,8,1,8,2304]{4,3,2,1,0:T(8,128)S(1)}, f32[1,8,1,8,2304]{4,3,2,1,0:T(8,128)}, u32[]{:S(2)}) %copy-start) | copy-done | bytes 589848
  2.5 0.0 copy-start.1
  2.5 0.9 %copy-done.1 = f32[1,1,8,2304]{3,2,1,0:T(8,128)S(1)} copy-done((f32[1,1,8,2304]{3,2,1,0:T(8,128)S(1)}, f32[1,1,8,2304]{3,2,1,0:T(8,128)}, u32[]{:S(2)}) %copy-start.1) | copy-done | bytes 73752
  3.4 0.0 copy-start.2
  3.4 0.9 %copy-done.2 = f32[1,1,8,2304]{3,2,1,0:T(8,128)S(1)} copy-done((f32[1,1,8,2304]{3,2,1,0:T(8,128)S(1)}, f32[1,1,8,2304]{3,2,1,0:T(8,128)}, u32[]{:S(2)}) %copy-start.2) | copy-done | bytes 73752
  4.3 0.0 copy-start.3
  4.3 0.9 %copy-done.3 = f32[1,1,8,2304]{3,2,1,0:T(8,128)S(1)} copy-done((f32[1,1,8,2304]{3,2,1,0:T(8,128)S(1)}, f32[1,1,8,2304]{3,2,1,0:T(8,128)}, u32[]{:S(2)}) %copy-start.3) | copy-done | bytes 73752
  5.2 0.0 copy-start.6
  5.2 0.7 copy-done.6
  5.9 0.0 copy-start.7
  5.9 0.7 copy-done.7
  6.6 67.5 %shard_map.100 = f32[8,8,2304]{2,1,0:T(8,128)S(1)} custom-call(f32[8,8,2304]{2,1,0:T(8,128)S(1)} %bitcast.5, f32[1,1,8,2304]{3,2,1,0:T(8,128)S(1)} %copy-done.1, f32[1,1,8,2304]{3,2,1,0:T(8,128)S(1)} %copy-done.2, f32[1,1,8,2304]{3,2,1,0:T(8,128)S(1)} %copy-done.3, f32[3,8,4]{2,1,0:T(8,128)S(1)} %copy.11.rs_ref, f32[4,8,8]{2,1,0:T(8,128)S(1)} %copy-done.4, ...), custom_call_target="tpu_custom_call" | custom-call | flops 8000000 | bytes 1500000 | tf_op jit(solution)/shard_map/pallas_call | solution.py:610
  74.0 0.8 %copy.15 = f32[1,8,1,8,2304]{4,3,2,1,0:T(8,128)} copy(f32[1,8,1,8,2304]{4,3,2,1,0:T(8,128)S(1)} %bitcast.4) | data formatting | bytes 1179648
Async XLA Ops:
  0.0 1.5 %copy-start.4 = (f32[4,8,8]{2,1,0:T(8,128)S(1)}, f32[4,8,8]{2,1,0:T(8,128)}, u32[]{:S(2)}) copy-start(f32[4,8,8]{2,1,0:T(8,128)} %fc_ref.1) | copy-start | bytes 3076
  0.7 0.8 %copy-start.5 = (s32[1,1,896]{2,1,0:T(1,128)S(1)}, s32[1,1,896]{2,1,0:T(1,128)}, u32[]{:S(2)}) copy-start(s32[1,1,896]{2,1,0:T(1,128)} %tgt_hbm.1) | copy-start | bytes 10756
  1.5 1.1 %copy-start = (f32[1,8,1,8,2304]{4,3,2,1,0:T(8,128)S(1)}, f32[1,8,1,8,2304]{4,3,2,1,0:T(8,128)}, u32[]{:S(2)}) copy-start(f32[1,8,1,8,2304]{4,3,2,1,0:T(8,128)} %param.10) | copy-start | bytes 1769476
  2.5 0.9 %copy-start.1 = (f32[1,1,8,2304]{3,2,1,0:T(8,128)S(1)}, f32[1,1,8,2304]{3,2,1,0:T(8,128)}, u32[]{:S(2)}) copy-start(f32[1,1,8,2304]{3,2,1,0:T(8,128)} %kap_hbm.1) | copy-start | bytes 221188
  3.4 0.9 %copy-start.2 = (f32[1,1,8,2304]{3,2,1,0:T(8,128)S(1)}, f32[1,1,8,2304]{3,2,1,0:T(8,128)}, u32[]{:S(2)}) copy-start(f32[1,1,8,2304]{3,2,1,0:T(8,128)} %vt_hbm.1) | copy-start | bytes 221188
  4.3 0.9 %copy-start.3 = (f32[1,1,8,2304]{3,2,1,0:T(8,128)S(1)}, f32[1,1,8,2304]{3,2,1,0:T(8,128)}, u32[]{:S(2)}) copy-start(f32[1,1,8,2304]{3,2,1,0:T(8,128)} %vp_hbm.1) | copy-start | bytes 221188
  5.2 0.7 copy-start.6
  5.9 0.7 copy-start.7

commit v3 on v2

--- a/solution.py
+++ b/solution.py
@@ -34,6 +34,7 @@
     don_hbm,
     wt_hbm,
     cnt_ref,
+    out_hbm,
     out_ref,
     c_ref,
     coef,
@@ -62,6 +63,7 @@
     rad_part,
     hal_part,
     load_sem,
+    store_sem,
     rad_ssem,
     rad_rsem,
     hal_ssem,
@@ -154,7 +156,7 @@
 
     def rad_copy(ph, src, up, k):
         slot = 0 if up else 1
-        cols = pl.ds(k * width, width)
+        cols = pl.ds(k * width if isinstance(k, int) else pl.multiple_of(k * width, width), width)
         return remote(
             src.at[:, :, cols],
             rad_buf.at[ph, slot, :, :, cols],
@@ -165,7 +167,7 @@
 
     def hal_copy(ph, down, k):
         slot = 0 if down else 1
-        cols = pl.ds(k * width, width)
+        cols = pl.ds(k * width if isinstance(k, int) else pl.multiple_of(k * width, width), width)
         return remote(
             hal_send.at[ph, slot, :, cols],
             hal_recv.at[ph, slot, :, cols],
@@ -276,6 +278,39 @@
             @pl.when(present)
             def _():
                 copy().start()
+
+    def sent_chunk(ph, src, k):
+        for present, copy in (
+            (has_high, lambda: rad_copy(ph, src, True, k)),
+            (has_low, lambda: rad_copy(ph, src, False, k)),
+            (has_south, lambda: hal_copy(ph, True, k)),
+            (has_north, lambda: hal_copy(ph, False, k)),
+        ):
+
+            @pl.when(present)
+            def _():
+                copy().wait_send()
+
+    class Stream:
+        def __init__(self, ph, src):
+            self.ph, self.src, self.begun, self.ended = ph, src, 0, 0
+            self.begin()
+            self.begin()
+
+        def begin(self):
+            if self.begun < chunks:
+                send_chunk(self.ph, self.src, self.begun)
+                self.begun += 1
+
+        def step(self):
+            if self.ended < self.begun:
+                sent_chunk(self.ph, self.src, self.ended)
+                self.ended += 1
+                self.begin()
+
+        def finish(self):
+            while self.ended < self.begun:
+                self.step()
 
     def wait_chunk(ph, src, k):
         for present, copy in (
@@ -374,13 +409,13 @@
         )
 
     def coefficients(f):
-        low = rs_ref[1, f, jnp.maximum(rad - 1, 0)]
-        high = rs_ref[2, f, jnp.minimum(rad + 1, levels - 1)]
+        low = rs_ref[1, jnp.maximum(rad - 1, 0), f]
+        high = rs_ref[2, jnp.minimum(rad + 1, levels - 1), f]
         low = jnp.where(has_low, low, F32(0.0))
         high = jnp.where(has_high, high, F32(0.0))
         return low, high
 
-    def overset(ph, src):
+    def overset(ph, src, stream):
         sides_all(ph).wait_recv()
         piece_copy(ph, 0, 0).wait_recv()
         piece_copy(ph, 1, 0).wait_recv()
@@ -395,7 +430,9 @@
         def _():
             val_copy(ph, False).start()
 
+        stream.step()
         scatter(values, own_part)
+        stream.step()
 
         def one(block, carry):
             at = pl.multiple_of(block * BLK, BLK)
@@ -409,6 +446,7 @@
         lax.fori_loop(0, nblk, one, 0)
         scatter_row(1, from_north)
         scatter_row(2, from_south)
+        stream.step()
 
         @pl.when(has_low)
         def _():
@@ -426,19 +464,7 @@
             )
         scatter(jnp.concatenate(mixed, axis=0), rad_part)
 
-    def wait_sends(ph, src):
-        for k in range(chunks):
-            for present, copy in (
-                (has_high, lambda: rad_copy(ph, src, True, k)),
-                (has_low, lambda: rad_copy(ph, src, False, k)),
-                (has_south, lambda: hal_copy(ph, True, k)),
-                (has_north, lambda: hal_copy(ph, False, k)),
-            ):
-
-                @pl.when(present)
-                def _():
-                    copy().wait_send()
-
+    def wait_sends(ph):
         for present, copy in (
             (has_high, lambda: val_copy(ph, True)),
             (has_low, lambda: val_copy(ph, False)),
@@ -481,7 +507,7 @@
                 mixed = low * rad_buf[ph, 0, f, :, cols] + high * rad_buf[ph, 1, f, :, cols]
                 acc = jnp.where(border, F32(0.0), mixed) + rad_part[pl.ds(start, rows), :]
                 acc = acc + south * below + north * above + west * before + east * after
-                acc = acc - center * cur + rs_ref[0, f, rad] * cur
+                acc = acc - center * cur + rs_ref[0, rad, f] * cur
                 here.append(cur)
                 total.append(acc)
             for e in range(fields):
@@ -491,55 +517,57 @@
                 finish(e, cols, at, here[e], acc)
             return carry
 
-        each = nblk // chunks
-        lax.fori_loop(k * each, (k + 1) * each, one, 0)
-
-    zero_block = jnp.zeros((2, fields, rows, 128), F32)
-    v_ref[:, :, :, 0:128] = zero_block
-    v_ref[:, :, :, columns + 128 : columns + 256] = zero_block
-    for present, slot in ((has_low, 0), (has_high, 1)):
-
-        @pl.when(jnp.logical_not(present))
-        def _():
-            for ph in range(2):
-                rad_buf[ph, slot] = jnp.zeros(rad_buf.shape[2:], F32)
-                val_recv[ph, slot] = jnp.zeros(val_recv.shape[2:], F32)
-
-    for present, slot in ((has_north, 0), (has_south, 1)):
-
-        @pl.when(jnp.logical_not(present))
-        def _():
-            info[1 + slot] = jnp.zeros(info.shape[1:], F32)
-            for ph in range(2):
-                hal_recv[ph, slot] = jnp.zeros(hal_recv.shape[2:], F32)
-
-    for load in loads:
+        return one(k, 0)
+
+    loads[0].wait()
+    pack_border(0, c_ref)
+
+    count = tiles
+    for present, _ in around:
+        count = count + jnp.where(present, 1, 0)
+    pl.semaphore_wait(barrier, count)
+    send_border(0)
+
+    for load in loads[1:]:
         load.wait()
     slot_ids = lax.broadcasted_iota(jnp.int32, (1, slots), 1)
     info[0, 0] = ints[0, 0].astype(F32)
     info[0, 1] = ints[1, 0].astype(F32)
     info[0, 2] = jnp.where(slot_ids < cnt_ref[0, 0], wts[0], F32(0.0))
+    for present, down in ((has_south, True), (has_north, False)):
+
+        @pl.when(present)
+        def _():
+            info_copy(down).start()
+
     for f in range(fields):
         hal_send[0, 0, f : f + 1, :] = c_ref[f, rows - 1 : rows, :]
         hal_send[0, 1, f : f + 1, :] = c_ref[f, 0:1, :]
-    pack_border(0, c_ref)
-
-    count = tiles
-    for present, _ in around:
-        count = count + jnp.where(present, 1, 0)
-    pl.semaphore_wait(barrier, count)
-
-    for present, down in ((has_south, True), (has_north, False)):
-
-        @pl.when(present)
-        def _():
-            info_copy(down).start()
-
-    send_chunk(0, c_ref, 0)
-    send_border(0)
-    for k in range(1, chunks):
-        send_chunk(0, c_ref, k)
+    stream = Stream(0, c_ref)
+
+    zero_block = jnp.zeros((2, fields, rows, 128), F32)
+    v_ref[:, :, :, 0:128] = zero_block
+    v_ref[:, :, :, columns + 128 : columns + 256] = zero_block
+    for present, slot in ((has_low, 0), (has_high, 1)):
+
+        @pl.when(jnp.logical_not(present))
+        def _():
+            for ph in range(2):
+                rad_buf[ph, slot] = jnp.zeros(rad_buf.shape[2:], F32)
+                val_recv[ph, slot] = jnp.zeros(val_recv.shape[2:], F32)
+
+    for present, slot in ((has_north, 0), (has_south, 1)):
+
+        @pl.when(jnp.logical_not(present))
+        def _():
+            info[1 + slot] = jnp.zeros(info.shape[1:], F32)
+            for ph in range(2):
+                hal_recv[ph, slot] = jnp.zeros(hal_recv.shape[2:], F32)
+
     prepare(0)
+    stream.step()
+    stream.step()
+    stream.step()
     for present, down in ((has_north, True), (has_south, False)):
 
         @pl.when(present)
@@ -548,7 +576,9 @@
 
     prepare(1)
     prepare(2)
-    overset(0, c_ref)
+    stream.step()
+    overset(0, c_ref, stream)
+    stream.finish()
 
     def pulled(e, cols, at, here, acc):
         value = STEP_SIZE * acc
@@ -556,32 +586,44 @@
         hal_send[1, 0, e : e + 1, cols] = value[rows - 1 : rows]
         hal_send[1, 1, e : e + 1, cols] = value[0:1]
 
-    for k in range(chunks):
+    def first(k, carry):
         wait_chunk(0, c_ref, k)
         operator(0, k, pulled)
-        if k == chunks - 1:
-            pack_border(1, w_ref)
-            send_border(1)
-        send_chunk(1, w_ref, k)
-
-    overset(1, w_ref)
+        return carry
+
+    lax.fori_loop(0, chunks, first, 0)
+    pack_border(1, w_ref)
+    send_border(1)
+    stream = Stream(1, w_ref)
+    for _ in range(3):
+        stream.step()
+    overset(1, w_ref, stream)
+    stream.finish()
 
     def final(e, cols, at, here, acc):
         out_ref[e, :, cols] = (
             v_ref[0, e, :, pl.ds(at + 128, BLK)] + here + (0.5 * STEP_SIZE) * acc
         )
 
-    for k in range(chunks):
+    def second(k, carry):
         wait_chunk(1, w_ref, k)
         operator(1, k, final)
+        cols = pl.ds(pl.multiple_of(k * width, width), width)
+        pltpu.make_async_copy(
+            out_ref.at[:, :, cols], out_hbm.at[:, :, cols], store_sem
+        ).start()
+        return carry
+
+    lax.fori_loop(0, chunks, second, 0)
     for present, down in ((has_south, True), (has_north, False)):
 
         @pl.when(present)
         def _():
             info_copy(down).wait_send()
 
-    wait_sends(0, c_ref)
-    wait_sends(1, w_ref)
+    wait_sends(0)
+    wait_sends(1)
+    pltpu.make_async_copy(out_ref, out_hbm, store_sem).wait()
 
 
 def body(
@@ -600,10 +642,9 @@
     tiles, levels = lax.axis_size("hor"), lax.axis_size("rad")
     slots = slot_targets.shape[-1]
     nblk = columns // BLK
-    chunks = 3 if nblk % 3 == 0 else 1
+    chunks = nblk
     window = -(-3 * (columns // tiles) // 128) * 128
     block = (fields, rows, columns)
-    vmem = pl.BlockSpec(memory_space=pltpu.VMEM)
     smem = pl.BlockSpec(memory_space=pltpu.SMEM)
     hbm = pl.BlockSpec(memory_space=pltpu.HBM)
     dma = pltpu.SemaphoreType.DMA
@@ -611,8 +652,9 @@
         functools.partial(kernel, tiles, levels, chunks),
         out_shape=jax.ShapeDtypeStruct(block, F32),
         in_specs=[hbm, hbm, hbm, hbm, smem, smem, hbm, hbm, hbm, smem],
-        out_specs=vmem,
+        out_specs=hbm,
         scratch_shapes=[
+            pltpu.VMEM(block, F32),
             pltpu.VMEM(block, F32),
             pltpu.VMEM((3, rows, columns), F32),
             pltpu.VMEM((2, 1, 1, slots), jnp.int32),
@@ -640,6 +682,7 @@
             pltpu.VMEM((nblk * fields * rows, BLK), F32),
             pltpu.VMEM((2, nblk * fields, BLK), F32),
             dma((7,)),
+            dma(()),
             dma((2, 2, chunks)),
             dma((2, 2, chunks)),
             dma((2, 2, chunks)),
@@ -654,7 +697,7 @@
             dma((2,)),
         ],
         compiler_params=pltpu.CompilerParams(
-            collective_id=0, has_side_effects=True, vmem_limit_bytes=48 * 2**20
+            collective_id=0, has_side_effects=True, vmem_limit_bytes=60 * 2**20
         ),
         cost_estimate=pl.CostEstimate(
             flops=8_000_000, bytes_accessed=1_500_000, transcendentals=0
@@ -664,7 +707,7 @@
         diffusivity,
         theta_velocity,
         phi_velocity,
-        radial_stencil,
+        jnp.swapaxes(radial_stencil, 1, 2),
         field_coupling,
         slot_targets,
         slot_donors,

time: 75.2 us -> 68.9 us (0.916)
  the two profiles are of different devices: /device:TPU:1 before, /device:TPU:32 now
where the time goes in v3:
time: 68.9 us; the launch traced here: 68.5 us
  Pallas kernels  65.9 us (96%)
  local copies, waits for them, and re-layouts  1.92 us (3%)
    pallas_call x1, Pallas kernels, body(): pl.pallas_call(functools.partial(kernel, tiles, levels, chunks), out_shap...  65.9 us
    unnamed x1, local copies, waits for them, and re-layouts  1.92 us

profile of v3, /device:TPU:32, one launch (start us, length us, event | category | flops | bytes accessed | tf_op | source)
XLA Modules:
  0.0 68.5 jit_solution(10616670452918417047)
XLA Ops:
  0.7 65.9 %shard_map.100 = f32[8,8,2304]{2,1,0:T(8,128)} custom-call(f32[8,8,2304]{2,1,0:T(8,128)} %bitcast.6, f32[1,1,8,2304]{3,2,1,0:T(8,128)} %kap_hbm.1, f32[1,1,8,2304]{3,2,1,0:T(8,128)} %vt_hbm.1, f32[1,1,8,2304]{3,2,1,0:T(8,128)} %vp_hbm.1, f32[3,4,8]{2,1,0:T(4,128)} %bitcast.7, f32[4,8,8]{2,1,0:T(8,128)} %fc_ref.1, s32[1,1,896]{2,1,0:T(1,128)} %tgt_hbm.1, ...), custom_call_target="tpu_custom_call" | custom-call | flops 8000000 | bytes 1500000 | tf_op jit(solution)/shard_map/pallas_call | solution.py:651
  66.6 1.9 %copy.14 = f32[1,8,1,8,2304]{4,3,2,1,0:T(8,128)} copy(f32[1,8,1,8,2304]{4,3,2,1,0:T(8,128)} %bitcast.5) | data formatting | bytes 1179648

commit v4 on v3

--- a/solution.py
+++ b/solution.py
@@ -12,6 +12,7 @@
 F32 = jnp.float32
 BF16 = jnp.bfloat16
 BLK = 256
+DEPTH = 2
 
 
 def split(x):
@@ -294,8 +295,8 @@
     class Stream:
         def __init__(self, ph, src):
             self.ph, self.src, self.begun, self.ended = ph, src, 0, 0
-            self.begin()
-            self.begin()
+            for _ in range(DEPTH):
+                self.begin()
 
         def begin(self):
             if self.begun < chunks:
@@ -578,7 +579,6 @@
     prepare(2)
     stream.step()
     overset(0, c_ref, stream)
-    stream.finish()
 
     def pulled(e, cols, at, here, acc):
         value = STEP_SIZE * acc
@@ -591,14 +591,18 @@
         operator(0, k, pulled)
         return carry
 
-    lax.fori_loop(0, chunks, first, 0)
+    cuts = [0, min(4, chunks), min(6, chunks), chunks]
+    lax.fori_loop(cuts[0], cuts[1], first, 0)
+    stream.step()
+    lax.fori_loop(cuts[1], cuts[2], first, 0)
+    stream.finish()
+    lax.fori_loop(cuts[2], cuts[3], first, 0)
     pack_border(1, w_ref)
     send_border(1)
     stream = Stream(1, w_ref)
     for _ in range(3):
         stream.step()
     overset(1, w_ref, stream)
-    stream.finish()
 
     def final(e, cols, at, here, acc):
         out_ref[e, :, cols] = (
@@ -614,7 +618,11 @@
         ).start()
         return carry
 
-    lax.fori_loop(0, chunks, second, 0)
+    lax.fori_loop(cuts[0], cuts[1], second, 0)
+    stream.step()
+    lax.fori_loop(cuts[1], cuts[2], second, 0)
+    stream.finish()
+    lax.fori_loop(cuts[2], cuts[3], second, 0)
     for present, down in ((has_south, True), (has_north, False)):
 
         @pl.when(present)

time: 68.9 us -> 68.9 us (level)
  no operation moved by 1% of the time
where the time goes in v4:
time: 68.9 us; the launch traced here: 68.2 us
  Pallas kernels  65.7 us (95%)
  local copies, waits for them, and re-layouts  1.92 us (3%)
    pallas_call x1, Pallas kernels, body(): pl.pallas_call(functools.partial(kernel, tiles, levels, chunks), out_shap...  65.7 us
    unnamed x1, local copies, waits for them, and re-layouts  1.92 us

profile of v4, /device:TPU:32, one launch (start us, length us, event | category | flops | bytes accessed | tf_op | source)
XLA Modules:
  0.0 68.2 jit_solution(1481779634505050616)
XLA Ops:
  0.7 65.7 %shard_map.100 = f32[8,8,2304]{2,1,0:T(8,128)} custom-call(f32[8,8,2304]{2,1,0:T(8,128)} %bitcast.6, f32[1,1,8,2304]{3,2,1,0:T(8,128)} %kap_hbm.1, f32[1,1,8,2304]{3,2,1,0:T(8,128)} %vt_hbm.1, f32[1,1,8,2304]{3,2,1,0:T(8,128)} %vp_hbm.1, f32[3,4,8]{2,1,0:T(4,128)} %bitcast.7, f32[4,8,8]{2,1,0:T(8,128)} %fc_ref.1, s32[1,1,896]{2,1,0:T(1,128)} %tgt_hbm.1, ...), custom_call_target="tpu_custom_call" | custom-call | flops 8000000 | bytes 1500000 | tf_op jit(solution)/shard_map/pallas_call | solution.py:659
  66.3 1.9 %copy.14 = f32[1,8,1,8,2304]{4,3,2,1,0:T(8,128)} copy(f32[1,8,1,8,2304]{4,3,2,1,0:T(8,128)} %bitcast.5) | data formatting | bytes 1179648
